TPU v7x, 32 devices: a whole 2x2x4 slice. The times are simulated.
32 devices in a mesh: pairs: 8 (over z, x), rep: 4 (over y, core).
Axes of the slice: x: 2, y: 2, z: 4, core: 2. Of those that a mesh axis runs over, the one named last changes fastest.
Arguments:
- factors: bfloat16 [8, 512, 512], P('pairs', 'rep'), may hold values from -1.1953125 to 1.1953125
- orbital_virtuals: bfloat16 [8, 512, 128], P('pairs'), may hold values from -0.25 to 0.25
- occupied: bfloat16 [8], P('pairs'), may hold values from -1.5 to -0.29882812
- pair_rotations: bfloat16 [256, 2, 128, 128], P('pairs'), may hold values from -0.5 to 0.5
- pair_energies: float32 [256, 2, 128], P('pairs'), may hold values from 0.5 to 4
- pair_orbitals: int32 [256, 2], P('pairs'), may hold values from 0 to 7
- pair_ranks: int32 [256], P('pairs'), may hold values from 32 to 128
- margins: bfloat16 [256, 6, 128, 128], P('pairs'), may hold values from -0.5 to 0.5
- coupling_weight: float32 [256, 6], P('pairs'), may hold values from -4 to 4
- send_slots: int32 [8, 8, 2], P('pairs'), may hold values from 0 to 31
- couplings: int32 [256, 6], P('pairs'), may hold values from 0 to 15
Outputs:
- amplitudes: bfloat16 [256, 128, 128], P('pairs')
- densities: float32 [8, 128, 128], P('pairs')
Inputs may be any that keep to these rules, and one draw needn't show every extreme that they name: `pair_orbitals`: the first and second orbital of a pair; they may be equal. `pair_ranks`: positions at or past a pair's rank are padding. send_slots[q, d, s] is the local pair, on index q of pairs, whose amplitudes fill slot s of what q sends to index d. `couplings`: entry k of a pair on index d names slot k % 2 of what index k // 2 sends to d.
All inputs are finite; a program needn't handle non-finite values.
Results may differ from a plain program's by a relative error of at most 0.0085.
Values may be sent and summed in bfloat16 or wider, within the bound.
A program may use at most 64 MiB of HBM per device.

v0:
```python
import jax
import jax.numpy as jnp
from jax import lax
from jax.sharding import PartitionSpec as P

ITERS = 3


def deliver(whole_amplitude, send_slots):
    slot_list = send_slots[0].reshape(-1)
    outgoing = jnp.take(whole_amplitude, slot_list, axis=0)
    arrived = lax.all_to_all(outgoing, "pairs", split_axis=0, concat_axis=0, tiled=True)
    return arrived


def relax_pairs(
    whole_amplitude,
    send_slots,
    integral,
    denominator,
    mask_pair,
    margin_rows,
    weight_rows,
    link_rows,
):
    arrived = deliver(whole_amplitude, send_slots)
    partner_amp = jnp.take(arrived, link_rows.reshape(-1), axis=0).reshape(
        link_rows.shape + arrived.shape[1:]
    )
    left_turn = jnp.einsum(
        "pcab,pcbd->pcad", margin_rows, partner_amp, preferred_element_type=jnp.float32
    ).astype(jnp.bfloat16)
    transformed = jnp.einsum(
        "pcad,pced->pcae", left_turn, margin_rows, preferred_element_type=jnp.float32
    )
    coupled = jnp.sum(weight_rows[:, :, None, None] * transformed, axis=1)
    return (-(integral - coupled) / denominator * mask_pair).astype(jnp.bfloat16)


def assemble(amplitude_part):
    return lax.all_gather(amplitude_part, "rep", axis=0, tiled=True)


def gram_pair(amplitude_rows, rotation_rows):
    side_left = jnp.einsum(
        "pxa,pab->pxb", rotation_rows[:, 0], amplitude_rows, preferred_element_type=jnp.float32
    ).astype(jnp.bfloat16)
    side_right = jnp.einsum(
        "pyb,pab->pya", rotation_rows[:, 1], amplitude_rows, preferred_element_type=jnp.float32
    ).astype(jnp.bfloat16)
    gram_left = jnp.einsum("pxb,pzb->pxz", side_left, side_left, preferred_element_type=jnp.float32)
    gram_right = jnp.einsum(
        "pxb,pzb->pxz", side_right, side_right, preferred_element_type=jnp.float32
    )
    return (gram_left, gram_right)


def body(
    factors,
    orbital_virtuals,
    occupied,
    pair_rotations,
    pair_energies,
    pair_orbitals,
    pair_ranks,
    margins,
    coupling_weight,
    send_slots,
    couplings,
):
    rank_size = pair_rotations.shape[-1]
    pair_count = pair_rotations.shape[0]
    orb_count = occupied.shape[0]
    rep_count = lax.axis_size("rep")
    halves = jnp.einsum(
        "oxp,opr->oxr", factors, orbital_virtuals, preferred_element_type=jnp.float32
    ).astype(jnp.bfloat16)
    aux_local = halves.shape[1]
    left_orbital = pair_orbitals[:, 0]
    right_orbital = pair_orbitals[:, 1]
    piece_half = lax.all_gather(halves, "pairs", axis=0, tiled=True)
    piece_occ = lax.all_gather(occupied, "pairs", axis=0, tiled=True)
    span_size = piece_half.shape[0]
    labels = jnp.arange(span_size, dtype=jnp.int32)
    pick_left = (left_orbital[:, None] == labels[None, :]).astype(jnp.bfloat16)
    pick_right = (right_orbital[:, None] == labels[None, :]).astype(jnp.bfloat16)
    flat_piece = piece_half.reshape(span_size, aux_local * rank_size)
    pick_both = pick_left.astype(jnp.float32) + pick_right.astype(jnp.float32)
    chosen_left = jnp.dot(pick_left, flat_piece, preferred_element_type=jnp.float32)
    chosen_right = jnp.dot(pick_right, flat_piece, preferred_element_type=jnp.float32)
    occ_pair = jnp.dot(pick_both, piece_occ.astype(jnp.float32), precision=lax.Precision.HIGHEST)
    half_left = chosen_left.astype(jnp.bfloat16).reshape(pair_count, aux_local, rank_size)
    half_right = chosen_right.astype(jnp.bfloat16).reshape(pair_count, aux_local, rank_size)
    mixed_pair = jnp.einsum(
        "pxa,pxb->pab", half_left, half_right, preferred_element_type=jnp.float32
    )
    rotations = pair_rotations.astype(jnp.float32)
    half_turn = jnp.einsum(
        "pxa,pxy->pay", rotations[:, 0], mixed_pair, precision=lax.Precision.HIGHEST
    )
    partial_value = jnp.einsum(
        "pay,pyb->pab", half_turn, rotations[:, 1], precision=lax.Precision.HIGHEST
    )
    positions = jnp.arange(rank_size, dtype=jnp.int32)
    visible = (positions[None, :] < pair_ranks[:, None]).astype(jnp.float32)
    mask_pair = visible[:, :, None] * visible[:, None, :]
    denominator = (
        pair_energies[:, 0, :, None] + pair_energies[:, 1, None, :] - occ_pair[:, None, None]
    )
    share_size = pair_count // rep_count
    offset = lax.axis_index("rep") * share_size

    def portion(values):
        return lax.dynamic_slice_in_dim(values, offset, share_size, 0)

    mask_part = portion(mask_pair)
    denominator_part = portion(denominator)
    integral = lax.psum_scatter(partial_value, "rep", scatter_dimension=0, tiled=True) * mask_part
    margin_part = portion(margins)
    weight_part = portion(coupling_weight)
    link_part = portion(couplings)
    amplitude = (-integral / denominator_part).astype(jnp.bfloat16)
    for iteration in range(ITERS):
        amplitude = relax_pairs(
            assemble(amplitude),
            send_slots,
            integral,
            denominator_part,
            mask_part,
            margin_part,
            weight_part,
            link_part,
        )
    final_amplitude = assemble(amplitude)
    gram_left, gram_right = gram_pair(final_amplitude, pair_rotations)
    flat_left = gram_left.reshape(pair_count, rank_size * rank_size)
    flat_right = gram_right.reshape(pair_count, rank_size * rank_size)
    labels = jnp.arange(lax.axis_size("pairs") * orb_count, dtype=jnp.int32)
    pick_left = (labels[:, None] == left_orbital[None, :]).astype(jnp.float32)
    pick_right = (labels[:, None] == right_orbital[None, :]).astype(jnp.float32)
    orbital_sum = jnp.dot(pick_left, flat_left, precision=lax.Precision.HIGHEST) + jnp.dot(
        pick_right, flat_right, precision=lax.Precision.HIGHEST
    )
    densities = lax.psum_scatter(
        (orbital_sum / rank_size).reshape(lax.axis_size("pairs") * orb_count, rank_size, rank_size),
        "pairs",
        scatter_dimension=0,
        tiled=True,
    )
    return (final_amplitude, densities)


def solution(mesh):
    return jax.shard_map(
        body,
        mesh=mesh,
        in_specs=(
            P("pairs", "rep", None),
            P("pairs", None, None),
            P("pairs"),
            P("pairs", None, None, None),
            P("pairs", None, None),
            P("pairs", None),
            P("pairs"),
            P("pairs", None, None, None),
            P("pairs", None),
            P("pairs", None, None),
            P("pairs", None),
        ),
        out_specs=(P("pairs", None, None), P("pairs", None, None)),
        check_vma=False,
    )
```

profile of v0, /device:TPU:0, one launch (start us, length us, event | category | flops | bytes accessed | tf_op | source)
XLA Modules:
  0.0 330.2 jit_solution(16679883421786389416)
XLA Ops:
  8.1 1.1 convolution_convert_fusion.7
  9.2 32.5 %all-gather = bf16[1024,128]{1,0:T(8,128)(2,1)S(1)} all-gather(bf16[128,128]{1,0:T(8,128)(2,1)S(1)} %convolution_convert_fusion.7), channel_id=2, replica_groups=mesh['pairs'=8,'rep'=4] {'pairs'}, dimensions={0}, use_global_device_ids=true | all-gather | bytes 294912 | tf_op jit(solution)/shard_map/all_gather | solution.py:81
  44.8 2.2 fusion.25
  47.1 2.5 fusion.21
  51.6 21.4 %all-reduce = bf16[8]{0:T(256)(128)(2,1)S(1)} all-reduce(bf16[8]{0:T(256)(128)(2,1)S(1)} %dynamic-update-slice), channel_id=1, replica_groups=mesh['pairs'=8,'rep'=4] {'pairs'}, use_global_device_ids=true, to_apply=%add | all-reduce | flops 8 | bytes 32
  73.4 8.7 %reduce-scatter.3.cloned.1.call-done = f32[8,128,128]{2,1,0:T(8,128)} async-done(((f32[32,128,128]{2,1,0:T(8,128)}), f32[8,128,128]{2,1,0:T(8,128)}) %reduce-scatter.3.cloned.1.call-update) | async-done | bytes 524304 | tf_op jit(solution)/shard_map/reduce_scatter | solution.py:118
  82.1 2.1 divide_convert_fusion
  84.5 16.7 %all-gather.6.cloned.1.call-done = bf16[32,128,128]{2,1,0:T(8,128)(2,1)} async-done(((bf16[8,128,128]{2,1,0:T(8,128)(2,1)}), bf16[32,128,128]{2,1,0:T(8,128)(2,1)}) %all-gather.6.cloned.1.call-update) | async-done | bytes 1048592 | tf_op jit(solution)/shard_map/all_gather | solution.py:41
  101.2 1.9 gather_fusion
  104.0 5.5 %all-to-all-start = ((bf16[16,128,128]{2,1,0:T(8,128)(2,1)}), bf16[16,128,128]{2,1,0:T(8,128)(2,1)S(1)}, u32[]{:S(2)}, u32[]{:S(2)}) async-start(bf16[16,128,128]{2,1,0:T(8,128)(2,1)} %broadcast_select_fusion.3), calls=%async_computation.1 | async-start | bytes 1048576 | tf_op jit(solution)/shard_map/all_to_all | solution.py:12
  110.0 14.4 %all-to-all-done = bf16[16,128,128]{2,1,0:T(8,128)(2,1)S(1)} async-done(((bf16[16,128,128]{2,1,0:T(8,128)(2,1)}), bf16[16,128,128]{2,1,0:T(8,128)(2,1)S(1)}, u32[]{:S(2)}, u32[]{:S(2)}) %all-to-all-start) | async-done | bytes 524320 | tf_op jit(solution)/shard_map/all_to_all | solution.py:12
  124.4 2.0 gather_fusion.1
  126.3 2.8 broadcast_select_fusion
  129.1 4.1 %multiply_reduce_fusion.2 = f32[8,128,128]{2,1,0:T(8,128)S(1)} fusion(f32[8,6]{1,0:T(8,128)S(1)} %copy.32, bf16[8,6,128,128]{3,2,1,0:T(8,128)(2,1)} %bitcast.71, bf16[32,6,128,128]{3,2,1,0:T(8,128)(2,1)} %param.22, s32[]{:T(128)S(6)} %select_n.21), kind=kOutput, calls=%fused_computation.12 | convolution fusion | flops 404881408 | bytes 5244096 | tf_op jit(solution)/shard_map/pcad,pced->pcae/dot_general | solution.py:33
  134.4 15.0 %all-gather.8.cloned.1.call-done = bf16[32,128,128]{2,1,0:T(8,128)(2,1)} async-done(((bf16[8,128,128]{2,1,0:T(8,128)(2,1)}), bf16[32,128,128]{2,1,0:T(8,128)(2,1)}) %all-gather.8.cloned.1.call-update) | async-done | bytes 1048592 | tf_op jit(solution)/shard_map/all_gather | solution.py:41
  149.3 1.9 gather_fusion.2
  151.3 20.2 %all_to_all.15 = bf16[16,128,128]{2,1,0:T(8,128)(2,1)S(1)} all-to-all(bf16[16,128,128]{2,1,0:T(8,128)(2,1)S(1)} %broadcast_select_fusion.4), channel_id=1, replica_groups=mesh['pairs'=8,'rep'=4] {'pairs'}, dimensions={0} | all-to-all | bytes 1048576 | tf_op jit(solution)/shard_map/all_to_all | solution.py:12
  171.5 2.0 gather_fusion.3
  173.5 2.8 broadcast_select_fusion.1
  176.3 4.1 %multiply_reduce_fusion.1 = f32[8,128,128]{2,1,0:T(8,128)S(1)} fusion(f32[8,6]{1,0:T(8,128)S(1)} %copy.32, bf16[8,6,128,128]{3,2,1,0:T(8,128)(2,1)} %bitcast.72, bf16[32,6,128,128]{3,2,1,0:T(8,128)(2,1)} %param.22, s32[]{:T(128)S(6)} %select_n.21), kind=kOutput, calls=%fused_computation.11 | convolution fusion | flops 404881408 | bytes 5244096 | tf_op jit(solution)/shard_map/pcad,pced->pcae/dot_general | solution.py:33
  181.5 15.0 %all-gather.10.cloned.1.call-done = bf16[32,128,128]{2,1,0:T(8,128)(2,1)} async-done(((bf16[8,128,128]{2,1,0:T(8,128)(2,1)}), bf16[32,128,128]{2,1,0:T(8,128)(2,1)}) %all-gather.10.cloned.1.call-update) | async-done | bytes 1048592 | tf_op jit(solution)/shard_map/all_gather | solution.py:41
  196.5 1.9 gather_fusion.4
  198.5 20.2 %all_to_all.16 = bf16[16,128,128]{2,1,0:T(8,128)(2,1)S(1)} all-to-all(bf16[16,128,128]{2,1,0:T(8,128)(2,1)S(1)} %broadcast_select_fusion.5), channel_id=1, replica_groups=mesh['pairs'=8,'rep'=4] {'pairs'}, dimensions={0} | all-to-all | bytes 1048576 | tf_op jit(solution)/shard_map/all_to_all | solution.py:12
  218.7 2.0 gather_fusion.5
  220.6 2.8 broadcast_select_fusion.2
  223.4 4.1 %multiply_reduce_fusion = f32[8,128,128]{2,1,0:T(8,128)S(1)} fusion(f32[8,6]{1,0:T(8,128)S(1)} %copy.32, bf16[8,6,128,128]{3,2,1,0:T(8,128)(2,1)} %bitcast.70, bf16[32,6,128,128]{3,2,1,0:T(8,128)(2,1)} %param.22, s32[]{:T(128)S(6)} %select_n.21), kind=kOutput, calls=%fused_computation.10 | convolution fusion | flops 404881408 | bytes 5244096 | tf_op jit(solution)/shard_map/pcad,pced->pcae/dot_general | solution.py:33
  228.7 15.0 %all-gather.12.cloned.1.call-done = bf16[32,128,128]{2,1,0:T(8,128)(2,1)} async-done(((bf16[8,128,128]{2,1,0:T(8,128)(2,1)}), bf16[32,128,128]{2,1,0:T(8,128)(2,1)}) %all-gather.12.cloned.1.call-update) | async-done | bytes 1048592 | tf_op jit(solution)/shard_map/all_gather | solution.py:41
  243.6 4.7 %fusion.7 = f32[32,128,128]{2,1,0:T(8,128)} fusion(bf16[32,128,128]{2,1,0:T(8,128)(2,1)} %all-gather.12.cloned.1.call-done, bf16[32,2,128,128]{3,2,1,0:T(8,128)(2,1)S(1)} %copy-done.3), kind=kOutput, calls=%fused_computation.27 | convolution fusion | flops 268959744 | bytes 4194304 | tf_op jit(solution)/shard_map/pxb,pzb->pxz/dot_general | solution.py:51
  248.3 4.3 %fusion.3 = f32[8,16384]{1,0:T(8,128)} fusion(f32[4,8,128,128]{3,2,1,0:T(8,128)} %bitcast.67, s32[32]{0:T(128)S(1)} %get-tuple-element.7), kind=kOutput, calls=%fused_computation.15 | convolution fusion | flops 50331904 | bytes 2621568 | tf_op jit(solution)/shard_map/dot_general | solution.py:141
  252.6 3.2 fusion.6
  255.8 3.5 %fusion.10 = f32[8,128,128]{2,0,1:T(8,128)S(1)} fusion(f32[8,16384]{1,0:T(8,128)} %fusion.3, f32[4,8,128,128]{3,2,1,0:T(8,128)} %bitcast.66, s32[32]{0:T(128)S(1)} %get-tuple-element.6), kind=kOutput, calls=%fused_computation.30 | convolution fusion | flops 50594048 | bytes 3145856 | tf_op jit(solution)/shard_map/dot_general | solution.py:141
  260.3 62.1 %reduce-scatter.5.cloned.1.call-done = f32[1,128,128]{2,1,0:T(8,128)} async-done(((f32[8,128,128]{2,1,0:T(8,128)}), f32[1,128,128]{2,1,0:T(8,128)}) %reduce-scatter.5.cloned.1.call-update) | async-done | bytes 65552 | tf_op jit(solution)/shard_map/reduce_scatter | solution.py:144
  (69 shorter events, 12.9 us)
Async XLA Ops:
  7.2 0.9 copy-start
  7.2 75.0 %reduce-scatter.3.cloned.1.call-start = ((), (), s32[]{:S(2)}) async-start(), calls=%async_computation.5 | async-start | bytes 2621440 | tf_op jit(solution)/shard_map/reduce_scatter | solution.py:118
  43.2 1.6 copy-start.3
  49.5 0.7 copy-start.9
  49.5 23.7 %copy-start.4 = (f32[32,2,128]{2,1,0:T(2,128)S(1)}, f32[32,2,128]{2,1,0:T(2,128)}, u32[]{:S(2)}) copy-start(f32[32,2,128]{2,1,0:T(2,128)} %param.19) | copy-start | bytes 98308
  49.5 23.8 %copy-start.8 = (s32[32]{0:T(128)S(1)}, s32[32]{0:T(128)}, u32[]{:S(2)}) copy-start(s32[32]{0:T(128)} %param.21) | copy-start | bytes 388
  49.5 34.7 %copy-start.7 = (s32[1,8,2]{1,2,0:T(2,128)S(1)}, s32[1,8,2]{1,2,0:T(2,128)}, u32[]{:S(2)}) copy-start(s32[1,8,2]{1,2,0:T(2,128)} %param.24) | copy-start | bytes 196
  49.6 51.6 %all-gather.6.cloned.1.call-start = ((), (), s32[]{:S(2)}) async-start(), calls=%async_computation.6 | async-start | bytes 1310720 | tf_op jit(solution)/shard_map/all_gather | solution.py:41
  82.1 27.4 %copy-start.5 = (s32[32,6]{0,1:T(8,128)S(1)}, s32[32,6]{0,1:T(8,128)}, u32[]{:S(2)}) copy-start(s32[32,6]{0,1:T(8,128)} %param.25) | copy-start | bytes 2308
  82.1 27.6 %copy-start.6 = (f32[32,6]{0,1:T(8,128)S(1)}, f32[32,6]{0,1:T(8,128)}, u32[]{:S(2)}) copy-start(f32[32,6]{0,1:T(8,128)} %param.23) | copy-start | bytes 2308
  104.0 20.4 %all-to-all-start = ((bf16[16,128,128]{2,1,0:T(8,128)(2,1)}), bf16[16,128,128]{2,1,0:T(8,128)(2,1)S(1)}, u32[]{:S(2)}, u32[]{:S(2)}) async-start(bf16[16,128,128]{2,1,0:T(8,128)(2,1)} %broadcast_select_fusion.3), calls=%async_computation.1 | async-start | bytes 1048576 | tf_op jit(solution)/shard_map/all_to_all | solution.py:12
  109.5 39.9 %all-gather.8.cloned.1.call-start = ((), (), s32[]{:S(2)}) async-start(), calls=%async_computation.7 | async-start | bytes 1310720 | tf_op jit(solution)/shard_map/all_gather | solution.py:41
  129.1 4.1 %copy-start.2 = (f32[8,128,128]{2,1,0:T(8,128)S(1)}, f32[8,128,128]{2,1,0:T(8,128)}, u32[]{:S(2)}) copy-start(f32[8,128,128]{2,1,0:T(8,128)} %reduce-scatter.3.cloned.1.call-done) | copy-start | bytes 1572868
  134.3 62.2 %all-gather.10.cloned.1.call-start = ((), (), s32[]{:S(2)}) async-start(), calls=%async_computation.8 | async-start | bytes 1310720 | tf_op jit(solution)/shard_map/all_gather | solution.py:41
  181.5 62.2 %all-gather.12.cloned.1.call-start = ((), (), s32[]{:S(2)}) async-start(), calls=%async_computation.9 | async-start | bytes 1310720 | tf_op jit(solution)/shard_map/all_gather | solution.py:41
  228.6 93.7 %reduce-scatter.5.cloned.1.call-start = ((), (), s32[]{:S(2)}) async-start(), calls=%async_computation.10 | async-start | bytes 589824 | tf_op jit(solution)/shard_map/reduce_scatter | solution.py:144
  248.3 4.3 %copy-start.1 = (bf16[32,128,128]{2,1,0:T(8,128)(2,1)S(1)}, bf16[32,128,128]{2,1,0:T(8,128)(2,1)}, u32[]{:S(2)}) copy-start(bf16[32,128,128]{2,1,0:T(8,128)(2,1)} %all-gather.12.cloned.1.call-done) | copy-start | bytes 3145732
Sparse Core Ops, SparseCore 0:
  49.7 32.3 reduce-scatter.2
  84.4 16.7 all-gather.5
  134.4 14.8 all-gather.7
  181.6 14.8 all-gather.9
  228.7 14.8 all-gather.11
  260.4 61.9 reduce-scatter.4
where the time goes:
time: 331 us; the launch traced here: 330 us
  waiting for transfers between devices  147 us (44%)
  blocking collectives  94.3 us (28%)
  matrix products  35.5 us (11%)
  local copies, waits for them, and re-layouts  17.9 us (5%)
  between operations  15 us (5%)
  other arithmetic  14.9 us (5%)
  starting transfers between devices  5.75 us (2%)
    reduce_scatter x1, waiting for transfers between devices, body(): lax.psum_scatter((orbital_sum / rank_size).reshape(lax.axis_size('pairs')...  62.1 us
    all_gather x4, waiting for transfers between devices, assemble(): return lax.all_gather(amplitude_part, 'rep', axis=0, tiled=True)  61.6 us
    all_to_all x2, blocking collectives, deliver(): lax.all_to_all(outgoing, 'pairs', split_axis=0, concat_axis=0, tiled=True)  40.4 us
    all_gather x1, blocking collectives, body(): piece_half = lax.all_gather(halves, 'pairs', axis=0, tiled=True)  32.5 us
    unnamed x1, blocking collectives  21.4 us
    all_to_all x1, waiting for transfers between devices, deliver(): lax.all_to_all(outgoing, 'pairs', split_axis=0, concat_axis=0, tiled=True)  14.4 us
    dot_general x3, matrix products, relax_pairs(): jnp.einsum('pcad,pced->pcae', left_turn, margin_rows, preferred_element_t...  12.4 us
    reduce_scatter x1, waiting for transfers between devices, body(): lax.psum_scatter(partial_value, 'rep', scatter_dimension=0, tiled=True)  8.7 us
  transfers between devices with their start and end apart: 7, of which 7 were waited for; matrix products, arithmetic and copies ran while one was open for 1% of the time, Pallas kernels for 0%

commit v1 on v0

v1 whole, which is shorter than its diff:
```python
import functools

import jax
import jax.numpy as jnp
from jax import lax
from jax.experimental import pallas as pl
from jax.experimental.pallas import tpu as pltpu
from jax.sharding import PartitionSpec as P

ITERS = 3
OCC_ROWS = 16
CHUNKS = 4
F32 = jnp.float32
BF16 = jnp.bfloat16


def dot_nn(a, b):
    return lax.dot_general(a, b, (((1,), (0,)), ((), ())), preferred_element_type=F32)


def dot_nt(a, b):
    return lax.dot_general(a, b, (((1,), (1,)), ((), ())), preferred_element_type=F32)


def two_parts(x):
    high = x.astype(BF16)
    low = (x - high.astype(F32)).astype(BF16)
    return jnp.concatenate([high, low], axis=0)


def kernel(
    groups,
    reps,
    factors_ref,
    virtuals_ref,
    occ_ref,
    energy_ref,
    orbitals_ref,
    ranks_ref,
    weight_ref,
    slots_ref,
    couplings_ref,
    rotations_hbm,
    margins_hbm,
    amp_ref,
    dens_ref,
    rot,
    margin,
    turn,
    halves,
    sbuf,
    slots,
    local,
    integ,
    scale,
    afin,
    grams,
    dsend1,
    drecv1,
    dsend2,
    drecv2,
    dfin,
    load_sem,
    s1,
    r1,
    ys,
    yr,
    ss,
    sr,
    fs,
    fr,
    d1s,
    d1r,
    d2s,
    d2r,
    d3s,
    d3r,
):
    me = lax.axis_index("pairs")
    rep = lax.axis_index("rep")
    sides = 2 if reps % 2 == 0 else 1
    lanes = reps // sides
    side = lax.rem(rep, sides)
    lane = rep // sides
    orbs, aux = factors_ref.shape[:2]
    pairs, _, rank, _ = rot.shape
    coups = margin.shape[1]
    rows = rank // reps
    capa = slots_ref.shape[1]
    norb = groups * orbs
    part = pairs // CHUNKS
    row0 = pl.multiple_of(rep * rows, rows)

    def lane_rep(step):
        return lax.rem(lane + step + lanes, lanes) * sides + side

    twin = lane * sides + (1 - side)

    def send(src, dst, ssem, rsem, group, to_rep):
        return pltpu.make_async_remote_copy(
            src_ref=src,
            dst_ref=dst,
            send_sem=ssem,
            recv_sem=rsem,
            device_id=(group, to_rep),
            device_id_type=pl.DeviceIdType.MESH,
        )

    rot_copy = pltpu.make_async_copy(rotations_hbm, rot, load_sem.at[0])
    rot_copy.start()
    margin_copy = pltpu.make_async_copy(margins_hbm, margin, load_sem.at[1])
    margin_copy.start()

    barrier = pltpu.get_barrier_semaphore()

    def greet(k, carry):
        pl.semaphore_signal(
            barrier,
            inc=1,
            device_id=(lax.rem(me + k, groups), rep),
            device_id_type=pl.DeviceIdType.MESH,
        )
        return carry

    lax.fori_loop(1, groups, greet, 0)
    for j in range(1, reps):
        pl.semaphore_signal(
            barrier,
            inc=1,
            device_id=(me, lax.rem(rep + j, reps)),
            device_id_type=pl.DeviceIdType.MESH,
        )

    for o in range(orbs):
        half = dot_nn(factors_ref[o], virtuals_ref[o]).astype(BF16)
        halves[rep, me * orbs + o, :aux, :] = half
        halves[rep, me * orbs + o, aux:, :] = occ_ref[o]

    rot_copy.wait()

    def flip(p, carry):
        turn[p] = rot[p, 0].astype(F32).T.astype(BF16)
        return carry

    lax.fori_loop(0, pairs, flip, 0, unroll=4)
    pl.semaphore_wait(barrier, groups - 1 + reps - 1)

    def group_copy(e, k, src, here):
        to = lax.rem(me + k, groups)
        return send(src(to), here(rep, me), s1.at[e, k], r1.at[e, k], to, rep)

    def lane_copy(e, j, k, here, q):
        block = here(rep, q)
        return send(block, block, ys.at[e, j, k], yr.at[e, j, k], me, lane_rep(j))

    def twin_copy(e, j, k, here, q):
        block = here(lane_rep(-j), q)
        return send(block, block, ss.at[e, j, k], sr.at[e, j, k], me, twin)

    def spread(e, src, here):
        def forward(k, carry):
            q = lax.rem(me - k + groups, groups)
            for j in range(1, lanes):
                lane_copy(e, j, k, here, q).start()
            if sides == 2:
                twin_copy(e, 0, k, here, q).start()
            return carry

        def arrive(k, carry):
            q = lax.rem(me - k + groups, groups)
            send(src(me), here(rep, q), s1.at[e, k], r1.at[e, k], me, rep).wait_recv()
            return forward(k, carry)

        def relay(k, carry):
            q = lax.rem(me - k + groups, groups)
            for j in range(1, lanes):
                block = here(lane_rep(-j), q)
                send(block, block, ys.at[e, j, k], yr.at[e, j, k], me, rep).wait_recv()
                if sides == 2:
                    twin_copy(e, j, k, here, q).start()
            return carry

        def settle(k, carry):
            q = lax.rem(me - k + groups, groups)
            for j in range(lanes):
                if sides == 2:
                    other = lax.rem(lane - j + lanes, lanes) * sides + (1 - side)
                    block = here(other, q)
                    send(block, block, ss.at[e, j, k], sr.at[e, j, k], me, rep).wait_recv()
            return carry

        def sent(k, carry):
            q = lax.rem(me - k + groups, groups)
            for j in range(1, lanes):
                lane_copy(e, j, k, here, q).wait_send()
            if sides == 2:
                for j in range(lanes):
                    twin_copy(e, j, k, here, q).wait_send()
            return carry

        def sent_group(k, carry):
            group_copy(e, k, src, here).wait_send()
            return carry

        forward(0, 0)
        lax.fori_loop(1, groups, arrive, 0)
        lax.fori_loop(0, groups, relay, 0)
        lax.fori_loop(0, groups, settle, 0)
        lax.fori_loop(0, groups, sent, 0)
        lax.fori_loop(1, groups, sent_group, 0)

    def half_place(r, q):
        return halves.at[r, pl.ds(q * orbs, orbs)]

    def half_source(d):
        return halves.at[rep, pl.ds(me * orbs, orbs)]

    def start_half(k, carry):
        group_copy(0, k, half_source, half_place).start()
        return carry

    lax.fori_loop(1, groups, start_half, 0)
    spread(0, half_source, half_place)

    row_at = lax.broadcasted_iota(jnp.int32, (rows, rank), 0) + row0
    column_at = lax.broadcasted_iota(jnp.int32, (rows, rank), 1)

    def integrate(p, carry):
        i = orbitals_ref[p, 0]
        j = orbitals_ref[p, 1]
        left = halves[:, i]
        right = halves[:, j]
        left_half = left[:, :aux].reshape(reps * aux, rank)
        right_half = right[:, :aux].reshape(reps * aux, rank)
        turned = two_parts(dot_nt(turn[p, pl.ds(row0, rows), :], left_half))
        mixed = dot_nn(turned, right_half)
        mixed = two_parts(mixed[:rows] + mixed[rows:])
        value = dot_nn(mixed, rot[p, 1])
        value = value[:rows] + value[rows:]
        occ = left[0, aux:].astype(F32)[:1] + right[0, aux:].astype(F32)[:1]
        live = (row_at < ranks_ref[0, p]) & (column_at < ranks_ref[0, p])
        factor = jnp.where(live, -1.0 / (energy_ref[p] - occ), 0.0)
        integ[p] = value
        scale[p] = factor
        local[p] = (value * factor).astype(BF16)
        return carry

    lax.fori_loop(0, pairs, integrate, 0, unroll=2)
    margin_copy.wait()

    def iterate(it, done):
        e = (it + 1) % 2

        def slot_place(r, q):
            return slots[it].at[r, pl.ds(q * capa, capa)]

        def slot_source(d):
            return sbuf.at[it, d]

        def post(k, carry):
            to = lax.rem(me + k, groups)
            for s in range(capa):
                sbuf[it, to, s] = local[slots_ref[to, s]]
            group_copy(e, k, slot_source, slot_place).start()
            return carry

        for s in range(capa):
            slots[it][rep, me * capa + s] = local[slots_ref[me, s]]
        lax.fori_loop(1, groups, post, 0)
        spread(e, slot_source, slot_place)

        def relax(p, carry):
            coupled = jnp.zeros((rows, rank), F32)
            for c in range(coups):
                amp = slots[it][:, couplings_ref[p, c]].reshape(rank, rank)
                left = dot_nn(margin[p, c, pl.ds(row0, rows), :], amp).astype(BF16)
                coupled = coupled + weight_ref[p, c] * dot_nt(left, margin[p, c])
            moved = ((integ[p] - coupled) * scale[p]).astype(BF16)
            if it == ITERS - 1:
                afin[rep, p] = moved
            else:
                local[p] = moved
            return carry

        for chunk in range(CHUNKS):
            lax.fori_loop(chunk * part, (chunk + 1) * part, relax, 0, unroll=2)
            done(chunk)

    for it in range(ITERS - 1):
        iterate(it, lambda chunk: None)

    def piece(r, chunk):
        return afin.at[r, pl.ds(chunk * part, part)]

    def final_lane(j, chunk):
        block = piece(rep, chunk)
        return send(block, block, fs.at[j, chunk], fr.at[j, chunk], me, lane_rep(j))

    def final_twin(j, chunk):
        block = piece(lane_rep(-j), chunk)
        index = lanes + j
        return send(block, block, fs.at[index, chunk], fr.at[index, chunk], me, twin)

    def publish(chunk):
        for j in range(1, lanes):
            final_lane(j, chunk).start()
        if sides == 2:
            final_twin(0, chunk).start()

    iterate(ITERS - 1, publish)

    for chunk in range(CHUNKS):
        for j in range(1, lanes):
            block = piece(lane_rep(-j), chunk)
            send(block, block, fs.at[j, chunk], fr.at[j, chunk], me, rep).wait_recv()
            if sides == 2:
                final_twin(j, chunk).start()
    for chunk in range(CHUNKS):
        if sides == 2:
            for j in range(lanes):
                other = lax.rem(lane - j + lanes, lanes) * sides + (1 - side)
                block = piece(other, chunk)
                index = lanes + j
                send(block, block, fs.at[index, chunk], fr.at[index, chunk], me, rep).wait_recv()

    def lay(p, carry):
        for r in range(reps):
            amp_ref[p, r * rows : (r + 1) * rows, :] = afin[r, p]
        return carry

    lax.fori_loop(0, pairs, lay, 0, unroll=4)

    share = pairs // reps
    base = rep * share

    def gram(k, carry):
        amp = afin[:, base + k].reshape(rank, rank)
        side_left = dot_nn(rot[base + k, 0], amp).astype(BF16)
        side_right = dot_nt(rot[base + k, 1], amp).astype(BF16)
        grams[2 * k] = dot_nt(side_left, side_left) * (1.0 / rank)
        grams[2 * k + 1] = dot_nt(side_right, side_right) * (1.0 / rank)
        return carry

    lax.fori_loop(0, share, gram, 0, unroll=2)

    def collect(o, carry):
        for r in range(reps):
            span = slice(r * rows, (r + 1) * rows)
            total = jnp.zeros((rows, rank), F32)
            for k in range(share):
                for s in range(2):
                    named = orbitals_ref[base + k, s] == o
                    total = total + jnp.where(named, grams[2 * k + s, span, :], 0.0)
            dsend1[r, o] = total.astype(BF16)
        return carry

    lax.fori_loop(0, norb, collect, 0)

    def density_rep(j):
        to = lax.rem(rep + j, reps)
        return send(dsend1.at[to], drecv1.at[rep], d1s.at[j], d1r.at[j], me, to)

    for j in range(1, reps):
        density_rep(j).start()
    drecv1[rep] = dsend1[rep]
    for j in range(1, reps):
        block = drecv1.at[lax.rem(rep - j + reps, reps)]
        send(block, block, d1s.at[j], d1r.at[j], me, rep).wait_recv()

    def density_group(k):
        to = lax.rem(me + k, groups)
        return send(dsend2.at[to], drecv2.at[me], d2s.at[k], d2r.at[k], to, rep)

    def rep_sum(d):
        total = jnp.zeros((orbs, rows, rank), F32)
        for r in range(reps):
            total = total + drecv1[r, pl.ds(d * orbs, orbs)].astype(F32)
        return total

    def post_density(k, carry):
        to = lax.rem(me + k, groups)
        dsend2[to] = rep_sum(to).astype(BF16)
        density_group(k).start()
        return carry

    lax.fori_loop(1, groups, post_density, 0)
    own = rep_sum(me)

    def take_density(k, total):
        q = lax.rem(me - k + groups, groups)
        block = drecv2.at[q]
        send(block, block, d2s.at[k], d2r.at[k], me, rep).wait_recv()
        return total + drecv2[q].astype(F32)

    dfin[rep] = lax.fori_loop(1, groups, take_density, own)

    def density_last(j):
        to = lax.rem(rep + j, reps)
        return send(dfin.at[rep], dfin.at[rep], d3s.at[j], d3r.at[j], me, to)

    for j in range(1, reps):
        density_last(j).start()
    for j in range(1, reps):
        block = dfin.at[lax.rem(rep - j + reps, reps)]
        send(block, block, d3s.at[j], d3r.at[j], me, rep).wait_recv()
    for r in range(reps):
        dens_ref[:, r * rows : (r + 1) * rows, :] = dfin[r]

    for chunk in range(CHUNKS):
        for j in range(1, lanes):
            final_lane(j, chunk).wait_send()
        if sides == 2:
            for j in range(lanes):
                final_twin(j, chunk).wait_send()
    for j in range(1, reps):
        density_rep(j).wait_send()
        density_last(j).wait_send()

    def sent_density(k, carry):
        density_group(k).wait_send()
        return carry

    lax.fori_loop(1, groups, sent_density, 0)


def body(
    factors,
    orbital_virtuals,
    occupied,
    pair_rotations,
    pair_energies,
    pair_orbitals,
    pair_ranks,
    margins,
    coupling_weight,
    send_slots,
    couplings,
):
    groups = lax.axis_size("pairs")
    reps = lax.axis_size("rep")
    orbs, aux, _ = factors.shape
    pairs, _, rank, _ = pair_rotations.shape
    coups = margins.shape[1]
    capa = send_slots.shape[2]
    rows = rank // reps
    norb = groups * orbs
    share = pairs // reps
    sides = 2 if reps % 2 == 0 else 1
    lanes = reps // sides
    own_rows = lax.dynamic_slice_in_dim(
        pair_energies[:, 0], lax.axis_index("rep") * rows, rows, 1
    )
    energy = own_rows[:, :, None] + pair_energies[:, 1][:, None, :]
    occ = jnp.broadcast_to(occupied[:, None, None], (orbs, OCC_ROWS, rank))
    vmem = pl.BlockSpec(memory_space=pltpu.VMEM)
    smem = pl.BlockSpec(memory_space=pltpu.SMEM)
    anywhere = pl.BlockSpec(memory_space=pl.ANY)
    dma = pltpu.SemaphoreType.DMA
    return pl.pallas_call(
        functools.partial(kernel, groups, reps),
        out_shape=(
            jax.ShapeDtypeStruct((pairs, rank, rank), BF16),
            jax.ShapeDtypeStruct((orbs, rank, rank), F32),
        ),
        in_specs=[vmem] * 4 + [smem] * 5 + [anywhere] * 2,
        out_specs=(vmem, vmem),
        scratch_shapes=[
            pltpu.VMEM(pair_rotations.shape, BF16),
            pltpu.VMEM(margins.shape, BF16),
            pltpu.VMEM((pairs, rank, rank), BF16),
            pltpu.VMEM((reps, norb, aux + OCC_ROWS, rank), BF16),
            pltpu.VMEM((ITERS, groups, capa, rows, rank), BF16),
            tuple(
                pltpu.VMEM((reps, groups * capa, rows, rank), BF16) for _ in range(ITERS)
            ),
            pltpu.VMEM((pairs, rows, rank), BF16),
            pltpu.VMEM((pairs, rows, rank), F32),
            pltpu.VMEM((pairs, rows, rank), F32),
            pltpu.VMEM((reps, pairs, rows, rank), BF16),
            pltpu.VMEM((2 * share, rank, rank), F32),
            pltpu.VMEM((reps, norb, rows, rank), BF16),
            pltpu.VMEM((reps, norb, rows, rank), BF16),
            pltpu.VMEM((groups, orbs, rows, rank), BF16),
            pltpu.VMEM((groups, orbs, rows, rank), BF16),
            pltpu.VMEM((reps, orbs, rows, rank), F32),
            dma((2,)),
            dma((2, groups)),
            dma((2, groups)),
            dma((2, lanes, groups)),
            dma((2, lanes, groups)),
            dma((2, lanes, groups)),
            dma((2, lanes, groups)),
            dma((2 * lanes, CHUNKS)),
            dma((2 * lanes, CHUNKS)),
            dma((reps,)),
            dma((reps,)),
            dma((groups,)),
            dma((groups,)),
            dma((reps,)),
            dma((reps,)),
        ],
        compiler_params=pltpu.CompilerParams(
            collective_id=0, has_side_effects=True, vmem_limit_bytes=60 * 1024 * 1024
        ),
        cost_estimate=pl.CostEstimate(
            flops=4 * pairs * coups * ITERS * rows * rank * rank,
            bytes_accessed=2 * pairs * coups * rank * rank,
            transcendentals=0,
        ),
    )(
        factors,
        orbital_virtuals,
        occ,
        energy,
        pair_orbitals,
        pair_ranks[None, :],
        coupling_weight,
        send_slots[0],
        couplings,
        pair_rotations,
        margins,
    )


def solution(mesh):
    return jax.shard_map(
        body,
        mesh=mesh,
        in_specs=(
            P("pairs", "rep", None),
            P("pairs", None, None),
            P("pairs"),
            P("pairs", None, None, None),
            P("pairs", None, None),
            P("pairs", None),
            P("pairs"),
            P("pairs", None, None, None),
            P("pairs", None),
            P("pairs", None, None),
            P("pairs", None),
        ),
        out_specs=(P("pairs", None, None), P("pairs", None, None)),
        check_vma=False,
    )
```

time: 331 us -> 139 us (0.42)
  waiting for transfers between devices: 147 us -> 0 us
  Pallas kernels: 0 us -> 126 us
  blocking collectives: 94.3 us -> 0 us
  matrix products: 35.5 us -> 0 us
  other arithmetic: 14.9 us -> 1 us
  between operations: 15 us -> 1.31 us
  local copies, waits for them, and re-layouts: 17.9 us -> 10.8 us
  starting transfers between devices: 5.75 us -> 0 us
    pallas_call x0 -> x1, Pallas kernels: none -> 126 us  [body(): pl.pallas_call(functools.partial(kernel, groups, reps), out_shape=(jax.Sh...]
    reduce_scatter x2 -> x0, waiting for transfers between devices: 70.8 us -> none  [the longest x1 62.1 us: body(): lax.psum_scatter((orbital_sum / rank_size).reshape(lax.axis_size('pairs')...]
    all_gather x4 -> x0, waiting for transfers between devices: 61.6 us -> none  [assemble(): return lax.all_gather(amplitude_part, 'rep', axis=0, tiled=True)]
    all_to_all x2 -> x0, blocking collectives: 40.4 us -> none  [deliver(): lax.all_to_all(outgoing, 'pairs', split_axis=0, concat_axis=0, tiled=True)]
    dot_general x14 -> x0, matrix products: 35.5 us -> none  [the longest x3 12.4 us: relax_pairs(): jnp.einsum('pcad,pced->pcae', left_turn, margin_rows, preferred_element_t...]
    all_gather x1 -> x0, blocking collectives: 32.5 us -> none  [body(): piece_half = lax.all_gather(halves, 'pairs', axis=0, tiled=True)]
    unnamed x1 -> x0, blocking collectives: 21.4 us -> none
    all_to_all x1 -> x0, waiting for transfers between devices: 14.4 us -> none  [deliver(): lax.all_to_all(outgoing, 'pairs', split_axis=0, concat_axis=0, tiled=True)]
  transfers between devices with their start and end apart: 7 -> 0, of which waited for: 7 -> 0; matrix products, arithmetic and copies ran while one was open for 1% -> 0% of each run, Pallas kernels for 0% -> 0%
where the time goes in v1:
time: 139 us
  Pallas kernels  126 us (91%)
  local copies, waits for them, and re-layouts  10.8 us (8%)
    pallas_call x1, Pallas kernels, body(): pl.pallas_call(functools.partial(kernel, groups, reps), out_shape=(jax.Sh...  126 us
    unnamed x5, local copies, waits for them, and re-layouts  7.88 us

profile of v1, /device:TPU:0, one launch (start us, length us, event | category | flops | bytes accessed | tf_op | source)
XLA Modules:
  0.0 139.0 jit_solution(9210153529604332868)
XLA Ops:
  1.3 0.6 broadcast_in_dim.13.occ_ref
  1.9 1.3 copy.15.slots_ref
  3.2 1.4 copy.13.orbitals_ref
  4.6 1.4 copy.14.weight_ref
  6.0 1.4 copy.16.couplings_ref
  7.3 0.9 fusion
  8.2 0.1 constant_dynamic-slice_fusion
  8.3 1.0 broadcast_add_fusion.energy_ref
  9.3 125.9 %shard_map.122 = (bf16[32,128,128]{2,1,0:T(8,128)(2,1)}, f32[1,128,128]{2,1,0:T(8,128)}) custom-call(bf16[1,128,512]{2,1,0:T(8,128)(2,1)} %factors_ref.1, bf16[1,512,128]{2,1,0:T(8,128)(2,1)} %virtuals_ref.1, bf16[1,16,128]{2,1,0:T(8,128)(2,1)} %broadcast_in_dim.13.occ_ref, f32[32,32,128]{2,1,0:T(8,128)} %broadcast_add_fusion.energy_ref, ...), custom_call_target="tpu_custom_call" | custom-call | flops 1207959552 | bytes 6291456 | tf_op jit(solution)/shard_map/pallas_call | solution.py:459
  135.2 2.3 %copy.20 = bf16[32,128,128]{2,1,0:T(8,128)(2,1)} copy(bf16[32,128,128]{2,1,0:T(8,128)(2,1)} %get-tuple-element.6) | data formatting | bytes 2097152
  137.5 1.5 %copy.21 = f32[1,128,128]{2,1,0:T(8,128)} copy(f32[1,128,128]{2,1,0:T(8,128)} %get-tuple-element.7) | data formatting | bytes 131072

commit v2 on v1

--- a/solution.py
+++ b/solution.py
@@ -9,7 +9,7 @@
 
 ITERS = 3
 OCC_ROWS = 16
-CHUNKS = 4
+UNROLL = 8
 F32 = jnp.float32
 BF16 = jnp.bfloat16
 
@@ -34,7 +34,7 @@
     factors_ref,
     virtuals_ref,
     occ_ref,
-    energy_ref,
+    energies_ref,
     orbitals_ref,
     ranks_ref,
     weight_ref,
@@ -86,9 +86,9 @@
     pairs, _, rank, _ = rot.shape
     coups = margin.shape[1]
     rows = rank // reps
-    capa = slots_ref.shape[1]
+    capa = slots_ref.shape[0]
     norb = groups * orbs
-    part = pairs // CHUNKS
+    share = pairs // reps
     row0 = pl.multiple_of(rep * rows, rows)
 
     def lane_rep(step):
@@ -133,126 +133,161 @@
 
     for o in range(orbs):
         half = dot_nn(factors_ref[o], virtuals_ref[o]).astype(BF16)
-        halves[rep, me * orbs + o, :aux, :] = half
-        halves[rep, me * orbs + o, aux:, :] = occ_ref[o]
-
-    rot_copy.wait()
-
-    def flip(p, carry):
-        turn[p] = rot[p, 0].astype(F32).T.astype(BF16)
-        return carry
-
-    lax.fori_loop(0, pairs, flip, 0, unroll=4)
+        level = jnp.broadcast_to(occ_ref[o : o + 1].astype(F32), (OCC_ROWS, rank))
+        halves[0][me * orbs + o, :aux, :] = half
+        halves[0][me * orbs + o, aux:, :] = level.astype(BF16)
+
     pl.semaphore_wait(barrier, groups - 1 + reps - 1)
 
     def group_copy(e, k, src, here):
         to = lax.rem(me + k, groups)
-        return send(src(to), here(rep, me), s1.at[e, k], r1.at[e, k], to, rep)
-
-    def lane_copy(e, j, k, here, q):
-        block = here(rep, q)
-        return send(block, block, ys.at[e, j, k], yr.at[e, j, k], me, lane_rep(j))
-
-    def twin_copy(e, j, k, here, q):
-        block = here(lane_rep(-j), q)
-        return send(block, block, ss.at[e, j, k], sr.at[e, j, k], me, twin)
-
-    def spread(e, src, here):
+        return send(src(to), here(0, 0, me), s1.at[e, k], r1.at[e, k], to, rep)
+
+    def spread(e, src, here, land, between, ready):
+        def source(k):
+            return lax.rem(me - k + groups, groups)
+
+        def lane_copy(j, k):
+            q = source(k)
+            return send(
+                here(0, 0, q), land(j, 0, q), ys.at[e, j, k], yr.at[e, j, k], me, lane_rep(j)
+            )
+
+        def twin_copy(j, k):
+            q = source(k)
+            return send(here(j, 0, q), land(j, 1, q), ss.at[e, j, k], sr.at[e, j, k], me, twin)
+
+        def took(place, ssem, rsem):
+            send(place, place, ssem, rsem, me, twin).wait_recv()
+
         def forward(k, carry):
-            q = lax.rem(me - k + groups, groups)
             for j in range(1, lanes):
-                lane_copy(e, j, k, here, q).start()
+                lane_copy(j, k).start()
             if sides == 2:
-                twin_copy(e, 0, k, here, q).start()
+                twin_copy(0, k).start()
             return carry
 
         def arrive(k, carry):
-            q = lax.rem(me - k + groups, groups)
-            send(src(me), here(rep, q), s1.at[e, k], r1.at[e, k], me, rep).wait_recv()
+            between(k)
+            took(here(0, 0, source(k)), s1.at[e, k], r1.at[e, k])
             return forward(k, carry)
 
-        def relay(k, carry):
-            q = lax.rem(me - k + groups, groups)
+        forward(0, 0)
+        lax.fori_loop(1, groups, arrive, 0)
+        ready(0, 0)
+
+        for j in range(1, lanes):
+
+            def relay(k, carry, j=j):
+                took(here(j, 0, source(k)), ys.at[e, j, k], yr.at[e, j, k])
+                if sides == 2:
+                    twin_copy(j, k).start()
+                return carry
+
+            lax.fori_loop(0, groups, relay, 0)
+            ready(j, 0)
+
+        if sides == 2:
+            for j in range(lanes):
+
+                def settle(k, carry, j=j):
+                    took(here(j, 1, source(k)), ss.at[e, j, k], sr.at[e, j, k])
+                    return carry
+
+                lax.fori_loop(0, groups, settle, 0)
+                ready(j, 1)
+
+        def sent(k, carry):
             for j in range(1, lanes):
-                block = here(lane_rep(-j), q)
-                send(block, block, ys.at[e, j, k], yr.at[e, j, k], me, rep).wait_recv()
-                if sides == 2:
-                    twin_copy(e, j, k, here, q).start()
-            return carry
-
-        def settle(k, carry):
-            q = lax.rem(me - k + groups, groups)
-            for j in range(lanes):
-                if sides == 2:
-                    other = lax.rem(lane - j + lanes, lanes) * sides + (1 - side)
-                    block = here(other, q)
-                    send(block, block, ss.at[e, j, k], sr.at[e, j, k], me, rep).wait_recv()
-            return carry
-
-        def sent(k, carry):
-            q = lax.rem(me - k + groups, groups)
-            for j in range(1, lanes):
-                lane_copy(e, j, k, here, q).wait_send()
+                lane_copy(j, k).wait_send()
             if sides == 2:
                 for j in range(lanes):
-                    twin_copy(e, j, k, here, q).wait_send()
+                    twin_copy(j, k).wait_send()
             return carry
 
         def sent_group(k, carry):
             group_copy(e, k, src, here).wait_send()
             return carry
 
-        forward(0, 0)
-        lax.fori_loop(1, groups, arrive, 0)
-        lax.fori_loop(0, groups, relay, 0)
-        lax.fori_loop(0, groups, settle, 0)
-        lax.fori_loop(0, groups, sent, 0)
-        lax.fori_loop(1, groups, sent_group, 0)
-
-    def half_place(r, q):
-        return halves.at[r, pl.ds(q * orbs, orbs)]
+        def finish():
+            lax.fori_loop(0, groups, sent, 0)
+            lax.fori_loop(1, groups, sent_group, 0)
+
+        return finish
+
+    def half_place(j, t, q):
+        return halves[j * sides + t].at[pl.ds(q * orbs, orbs)]
 
     def half_source(d):
-        return halves.at[rep, pl.ds(me * orbs, orbs)]
+        return half_place(0, 0, me)
 
     def start_half(k, carry):
         group_copy(0, k, half_source, half_place).start()
         return carry
 
     lax.fori_loop(1, groups, start_half, 0)
-    spread(0, half_source, half_place)
+    rot_copy.wait()
+    flips = -(-pairs // max(groups - 1, 1))
+
+    def flip(k):
+        for step in range(flips):
+            p = jnp.minimum((k - 1) * flips + step, pairs - 1)
+            turn[p] = rot[p, 0].astype(F32).T.astype(BF16)
 
     row_at = lax.broadcasted_iota(jnp.int32, (rows, rank), 0) + row0
     column_at = lax.broadcasted_iota(jnp.int32, (rows, rank), 1)
 
-    def integrate(p, carry):
-        i = orbitals_ref[p, 0]
-        j = orbitals_ref[p, 1]
-        left = halves[:, i]
-        right = halves[:, j]
-        left_half = left[:, :aux].reshape(reps * aux, rank)
-        right_half = right[:, :aux].reshape(reps * aux, rank)
-        turned = two_parts(dot_nt(turn[p, pl.ds(row0, rows), :], left_half))
-        mixed = dot_nn(turned, right_half)
-        mixed = two_parts(mixed[:rows] + mixed[rows:])
-        value = dot_nn(mixed, rot[p, 1])
-        value = value[:rows] + value[rows:]
-        occ = left[0, aux:].astype(F32)[:1] + right[0, aux:].astype(F32)[:1]
-        live = (row_at < ranks_ref[0, p]) & (column_at < ranks_ref[0, p])
-        factor = jnp.where(live, -1.0 / (energy_ref[p] - occ), 0.0)
-        integ[p] = value
-        scale[p] = factor
-        local[p] = (value * factor).astype(BF16)
-        return carry
-
-    lax.fori_loop(0, pairs, integrate, 0, unroll=2)
+    def integrate(j, t):
+        block = halves[j * sides + t]
+        last = j == lanes - 1 and t == sides - 1
+
+        def step(p, carry):
+            left = block[orbitals_ref[0, p]]
+            right = block[orbitals_ref[1, p]]
+            turned = two_parts(dot_nt(turn[p, pl.ds(row0, rows), :], left[:aux]))
+            mixed = dot_nn(turned, right[:aux])
+            mixed = mixed[:rows] + mixed[rows:]
+            if j or t:
+                mixed = mixed + integ[p]
+            if not last:
+                integ[p] = mixed
+                return carry
+            value = dot_nn(two_parts(mixed), rot[p, 1])
+            value = value[:rows] + value[rows:]
+            occ = left[aux:].astype(F32)[:1] + right[aux:].astype(F32)[:1]
+            first = energies_ref[p][:1]
+            second = energies_ref[p][1:]
+            first = jnp.sum(jnp.where(row_at == column_at, first, 0.0), axis=1, keepdims=True)
+            live = (row_at < ranks_ref[0, p]) & (column_at < ranks_ref[0, p])
+            factor = jnp.where(live, -1.0 / (first + second - occ), 0.0)
+            integ[p] = value
+            scale[p] = factor
+            local[p] = (value * factor).astype(BF16)
+            return carry
+
+        lax.fori_loop(0, pairs, step, 0, unroll=4 if last else UNROLL)
+
+    finish = spread(0, half_source, half_place, half_place, flip, integrate)
     margin_copy.wait()
-
-    def iterate(it, done):
+    finish()
+
+    def relax(it, p):
+        coupled = jnp.zeros((rows, rank), F32)
+        for c in range(coups):
+            amp = slots[it][:, couplings_ref[c, p]].reshape(rank, rank)
+            left = dot_nn(margin[p, c, pl.ds(row0, rows), :], amp).astype(BF16)
+            coupled = coupled + weight_ref[c, p] * dot_nt(left, margin[p, c])
+        return ((integ[p] - coupled) * scale[p]).astype(BF16)
+
+    def deliver(it):
         e = (it + 1) % 2
 
-        def slot_place(r, q):
-            return slots[it].at[r, pl.ds(q * capa, capa)]
+        def slot_place(j, t, q):
+            index = lax.rem(lane - j + lanes, lanes) * sides + (side if t == 0 else 1 - side)
+            return slots[it].at[index, pl.ds(q * capa, capa)]
+
+        def slot_land(j, t, q):
+            return slot_place(0 if t == 0 else j, 0, q)
 
         def slot_source(d):
             return sbuf.at[it, d]
@@ -260,37 +295,31 @@
         def post(k, carry):
             to = lax.rem(me + k, groups)
             for s in range(capa):
-                sbuf[it, to, s] = local[slots_ref[to, s]]
+                sbuf[it, to, s] = local[slots_ref[s, to]]
             group_copy(e, k, slot_source, slot_place).start()
             return carry
 
+        lax.fori_loop(1, groups, post, 0)
         for s in range(capa):
-            slots[it][rep, me * capa + s] = local[slots_ref[me, s]]
-        lax.fori_loop(1, groups, post, 0)
-        spread(e, slot_source, slot_place)
-
-        def relax(p, carry):
-            coupled = jnp.zeros((rows, rank), F32)
-            for c in range(coups):
-                amp = slots[it][:, couplings_ref[p, c]].reshape(rank, rank)
-                left = dot_nn(margin[p, c, pl.ds(row0, rows), :], amp).astype(BF16)
-                coupled = coupled + weight_ref[p, c] * dot_nt(left, margin[p, c])
-            moved = ((integ[p] - coupled) * scale[p]).astype(BF16)
-            if it == ITERS - 1:
-                afin[rep, p] = moved
-            else:
-                local[p] = moved
+            slots[it][rep, me * capa + s] = local[slots_ref[s, me]]
+        return spread(
+            e, slot_source, slot_place, slot_land, lambda k: None, lambda j, t: None
+        )
+
+    for it in range(ITERS - 1):
+        finish = deliver(it)
+
+        def step(p, carry, it=it):
+            local[p] = relax(it, p)
             return carry
 
-        for chunk in range(CHUNKS):
-            lax.fori_loop(chunk * part, (chunk + 1) * part, relax, 0, unroll=2)
-            done(chunk)
-
-    for it in range(ITERS - 1):
-        iterate(it, lambda chunk: None)
+        lax.fori_loop(0, pairs, step, 0, unroll=UNROLL)
+        finish()
+
+    finish = deliver(ITERS - 1)
 
     def piece(r, chunk):
-        return afin.at[r, pl.ds(chunk * part, part)]
+        return afin.at[r, pl.ds(chunk * share, share)]
 
     def final_lane(j, chunk):
         block = piece(rep, chunk)
@@ -301,36 +330,39 @@
         index = lanes + j
         return send(block, block, fs.at[index, chunk], fr.at[index, chunk], me, twin)
 
-    def publish(chunk):
-        for j in range(1, lanes):
-            final_lane(j, chunk).start()
-        if sides == 2:
-            final_twin(0, chunk).start()
-
-    iterate(ITERS - 1, publish)
-
-    for chunk in range(CHUNKS):
+    def relay_final(chunk):
         for j in range(1, lanes):
             block = piece(lane_rep(-j), chunk)
-            send(block, block, fs.at[j, chunk], fr.at[j, chunk], me, rep).wait_recv()
+            send(block, block, fs.at[j, chunk], fr.at[j, chunk], me, twin).wait_recv()
             if sides == 2:
                 final_twin(j, chunk).start()
-    for chunk in range(CHUNKS):
+
+    def settle_final(chunk):
         if sides == 2:
             for j in range(lanes):
                 other = lax.rem(lane - j + lanes, lanes) * sides + (1 - side)
                 block = piece(other, chunk)
                 index = lanes + j
-                send(block, block, fs.at[index, chunk], fr.at[index, chunk], me, rep).wait_recv()
-
-    def lay(p, carry):
-        for r in range(reps):
-            amp_ref[p, r * rows : (r + 1) * rows, :] = afin[r, p]
-        return carry
-
-    lax.fori_loop(0, pairs, lay, 0, unroll=4)
-
-    share = pairs // reps
+                send(block, block, fs.at[index, chunk], fr.at[index, chunk], me, twin).wait_recv()
+
+    def last_chunk(step, carry):
+        turn_lane = lax.rem(lane + 1 + step // sides, lanes)
+        turn_side = lax.rem(side + step, sides)
+        chunk = turn_lane * sides + turn_side
+        base = chunk * share
+        for k in range(share):
+            afin[rep, base + k] = relax(ITERS - 1, base + k)
+        for j in range(1, lanes):
+            final_lane(j, chunk).start()
+        if sides == 2:
+            final_twin(0, chunk).start()
+        return carry
+
+    lax.fori_loop(0, reps, last_chunk, 0)
+    if sides == 2:
+        relay_final(twin)
+    relay_final(rep)
+    settle_final(rep)
     base = rep * share
 
     def gram(k, carry):
@@ -349,7 +381,7 @@
             total = jnp.zeros((rows, rank), F32)
             for k in range(share):
                 for s in range(2):
-                    named = orbitals_ref[base + k, s] == o
+                    named = orbitals_ref[s, base + k] == o
                     total = total + jnp.where(named, grams[2 * k + s, span, :], 0.0)
             dsend1[r, o] = total.astype(BF16)
         return carry
@@ -363,6 +395,14 @@
     for j in range(1, reps):
         density_rep(j).start()
     drecv1[rep] = dsend1[rep]
+
+    def rest(step, carry):
+        relay_final(lax.rem(lane + step, lanes) * sides + side)
+        if sides == 2:
+            relay_final(lax.rem(lane + step, lanes) * sides + 1 - side)
+        return carry
+
+    lax.fori_loop(1, lanes, rest, 0)
     for j in range(1, reps):
         block = drecv1.at[lax.rem(rep - j + reps, reps)]
         send(block, block, d1s.at[j], d1r.at[j], me, rep).wait_recv()
@@ -394,19 +434,31 @@
 
     dfin[rep] = lax.fori_loop(1, groups, take_density, own)
 
+    def settle_rest(step, carry):
+        settle_final(lax.rem(rep + step, reps))
+        return carry
+
+    def lay(p, carry):
+        for r in range(reps):
+            amp_ref[p, r * rows : (r + 1) * rows, :] = afin[r, p]
+        return carry
+
     def density_last(j):
         to = lax.rem(rep + j, reps)
         return send(dfin.at[rep], dfin.at[rep], d3s.at[j], d3r.at[j], me, to)
 
     for j in range(1, reps):
         density_last(j).start()
+    lax.fori_loop(1, reps, settle_rest, 0)
+    lax.fori_loop(0, pairs, lay, 0, unroll=4)
     for j in range(1, reps):
         block = dfin.at[lax.rem(rep - j + reps, reps)]
         send(block, block, d3s.at[j], d3r.at[j], me, rep).wait_recv()
     for r in range(reps):
         dens_ref[:, r * rows : (r + 1) * rows, :] = dfin[r]
 
-    for chunk in range(CHUNKS):
+    finish()
+    for chunk in range(reps):
         for j in range(1, lanes):
             final_lane(j, chunk).wait_send()
         if sides == 2:
@@ -447,11 +499,6 @@
     share = pairs // reps
     sides = 2 if reps % 2 == 0 else 1
     lanes = reps // sides
-    own_rows = lax.dynamic_slice_in_dim(
-        pair_energies[:, 0], lax.axis_index("rep") * rows, rows, 1
-    )
-    energy = own_rows[:, :, None] + pair_energies[:, 1][:, None, :]
-    occ = jnp.broadcast_to(occupied[:, None, None], (orbs, OCC_ROWS, rank))
     vmem = pl.BlockSpec(memory_space=pltpu.VMEM)
     smem = pl.BlockSpec(memory_space=pltpu.SMEM)
     anywhere = pl.BlockSpec(memory_space=pl.ANY)
@@ -468,7 +515,7 @@
             pltpu.VMEM(pair_rotations.shape, BF16),
             pltpu.VMEM(margins.shape, BF16),
             pltpu.VMEM((pairs, rank, rank), BF16),
-            pltpu.VMEM((reps, norb, aux + OCC_ROWS, rank), BF16),
+            tuple(pltpu.VMEM((norb, aux + OCC_ROWS, rank), BF16) for _ in range(reps)),
             pltpu.VMEM((ITERS, groups, capa, rows, rank), BF16),
             tuple(
                 pltpu.VMEM((reps, groups * capa, rows, rank), BF16) for _ in range(ITERS)
@@ -490,8 +537,8 @@
             dma((2, lanes, groups)),
             dma((2, lanes, groups)),
             dma((2, lanes, groups)),
-            dma((2 * lanes, CHUNKS)),
-            dma((2 * lanes, CHUNKS)),
+            dma((2 * lanes, reps)),
+            dma((2 * lanes, reps)),
             dma((reps,)),
             dma((reps,)),
             dma((groups,)),
@@ -510,13 +557,13 @@
     )(
         factors,
         orbital_virtuals,
-        occ,
-        energy,
-        pair_orbitals,
+        occupied[:, None],
+        pair_energies,
+        pair_orbitals.T,
         pair_ranks[None, :],
-        coupling_weight,
-        send_slots[0],
-        couplings,
+        coupling_weight.T,
+        send_slots[0].T,
+        couplings.T,
         pair_rotations,
         margins,
     )

time: 139 us -> 128 us (0.921)
  local copies, waits for them, and re-layouts: 10.8 us -> 3.78 us
  Pallas kernels: 126 us -> 122 us
    unnamed x5 -> x2, local copies, waits for them, and re-layouts: 7.88 us -> 3.78 us
    pallas_call x1, Pallas kernels: 126 us -> 122 us  [body(): pl.pallas_call(functools.partial(kernel, groups, reps), out_shape=(jax.Sh...]
where the time goes in v2:
time: 128 us; the launch traced here: 127 us
  Pallas kernels  122 us (95%)
  local copies, waits for them, and re-layouts  3.78 us (3%)
  between operations  1.3 us (1%)
    pallas_call x1, Pallas kernels, body(): pl.pallas_call(functools.partial(kernel, groups, reps), out_shape=(jax.Sh...  122 us
    unnamed x2, local copies, waits for them, and re-layouts  3.78 us

profile of v2, /device:TPU:0, one launch (start us, length us, event | category | flops | bytes accessed | tf_op | source)
XLA Modules:
  0.0 127.5 jit_solution(4390014740547209791)
XLA Ops:
  1.3 122.4 %shard_map.122 = (bf16[32,128,128]{2,1,0:T(8,128)(2,1)}, f32[1,128,128]{2,1,0:T(8,128)}) custom-call(bf16[1,128,512]{2,1,0:T(8,128)(2,1)} %factors_ref.1, bf16[1,512,128]{2,1,0:T(8,128)(2,1)} %virtuals_ref.1, bf16[1,1]{1,0:T(2,128)(2,1)} %bitcast.8.occ_ref, f32[32,2,128]{2,1,0:T(2,128)} %energies_ref.1, s32[2,32]{1,0:T(2,128)} %bitcast.11, ...), custom_call_target="tpu_custom_call" | custom-call | flops 1207959552 | bytes 6291456 | tf_op jit(solution)/shard_map/pallas_call | solution.py:506
  123.7 2.3 %copy.16 = bf16[32,128,128]{2,1,0:T(8,128)(2,1)} copy(bf16[32,128,128]{2,1,0:T(8,128)(2,1)} %get-tuple-element.4) | data formatting | bytes 2097152
  126.0 1.5 %copy.17 = f32[1,128,128]{2,1,0:T(8,128)} copy(f32[1,128,128]{2,1,0:T(8,128)} %get-tuple-element.5) | data formatting | bytes 131072

commit v3 on v2

--- a/solution.py
+++ b/solution.py
@@ -26,6 +26,31 @@
     high = x.astype(BF16)
     low = (x - high.astype(F32)).astype(BF16)
     return jnp.concatenate([high, low], axis=0)
+
+
+def spaced(lhs):
+    zero = jnp.zeros_like(lhs[0])
+    sides = [[x, zero] if n % 2 == 0 else [zero, x] for n, x in enumerate(lhs)]
+    return jnp.concatenate([jnp.concatenate(x, axis=1) for x in sides], axis=0)
+
+
+def square(a, b, c, d):
+    return jnp.concatenate(
+        [jnp.concatenate([a, b], axis=1), jnp.concatenate([c, d], axis=1)], axis=0
+    )
+
+
+def apart(out):
+    rows, width = out.shape[0] // 4, out.shape[1] // 2
+    return [out[n * rows : (n + 1) * rows, (n // 2) * width :][:, :width] for n in range(4)]
+
+
+def four_nn(lhs, rhs):
+    return apart(dot_nn(spaced(lhs), square(rhs[0], rhs[2], rhs[1], rhs[3])))
+
+
+def four_nt(lhs, rhs):
+    return apart(dot_nt(spaced(lhs), square(rhs[0], rhs[1], rhs[2], rhs[3])))
 
 
 def kernel(
@@ -241,43 +266,60 @@
         block = halves[j * sides + t]
         last = j == lanes - 1 and t == sides - 1
 
-        def step(p, carry):
-            left = block[orbitals_ref[0, p]]
-            right = block[orbitals_ref[1, p]]
-            turned = two_parts(dot_nt(turn[p, pl.ds(row0, rows), :], left[:aux]))
-            mixed = dot_nn(turned, right[:aux])
-            mixed = mixed[:rows] + mixed[rows:]
+        def step(n, carry):
+            four = [4 * n + m for m in range(4)]
+            left = [block[orbitals_ref[0, p]] for p in four]
+            right = [block[orbitals_ref[1, p]] for p in four]
+            turned = four_nt(
+                [turn[p, pl.ds(row0, rows), :] for p in four], [x[:aux] for x in left]
+            )
+            mixed = four_nn([two_parts(x) for x in turned], [x[:aux] for x in right])
+            mixed = [x[:rows] + x[rows:] for x in mixed]
             if j or t:
-                mixed = mixed + integ[p]
+                mixed = [x + integ[p] for x, p in zip(mixed, four)]
             if not last:
-                integ[p] = mixed
+                for x, p in zip(mixed, four):
+                    integ[p] = x
                 return carry
-            value = dot_nn(two_parts(mixed), rot[p, 1])
-            value = value[:rows] + value[rows:]
-            occ = left[aux:].astype(F32)[:1] + right[aux:].astype(F32)[:1]
-            first = energies_ref[p][:1]
-            second = energies_ref[p][1:]
-            first = jnp.sum(jnp.where(row_at == column_at, first, 0.0), axis=1, keepdims=True)
-            live = (row_at < ranks_ref[0, p]) & (column_at < ranks_ref[0, p])
-            factor = jnp.where(live, -1.0 / (first + second - occ), 0.0)
-            integ[p] = value
-            scale[p] = factor
-            local[p] = (value * factor).astype(BF16)
+            values = four_nn([two_parts(x) for x in mixed], [rot[p, 1] for p in four])
+            for m, p in enumerate(four):
+                value = values[m][:rows] + values[m][rows:]
+                occ = left[m][aux:].astype(F32)[:1] + right[m][aux:].astype(F32)[:1]
+                first = energies_ref[p][:1]
+                second = energies_ref[p][1:]
+                first = jnp.sum(jnp.where(row_at == column_at, first, 0.0), axis=1, keepdims=True)
+                live = (row_at < ranks_ref[0, p]) & (column_at < ranks_ref[0, p])
+                factor = jnp.where(live, -1.0 / (first + second - occ), 0.0)
+                integ[p] = value
+                scale[p] = factor
+                local[p] = (value * factor).astype(BF16)
             return carry
 
-        lax.fori_loop(0, pairs, step, 0, unroll=4 if last else UNROLL)
+        lax.fori_loop(0, pairs // 4, step, 0, unroll=2)
 
     finish = spread(0, half_source, half_place, half_place, flip, integrate)
     margin_copy.wait()
     finish()
 
     def relax(it, p):
-        coupled = jnp.zeros((rows, rank), F32)
-        for c in range(coups):
-            amp = slots[it][:, couplings_ref[c, p]].reshape(rank, rank)
-            left = dot_nn(margin[p, c, pl.ds(row0, rows), :], amp).astype(BF16)
-            coupled = coupled + weight_ref[c, p] * dot_nt(left, margin[p, c])
-        return ((integ[p] - coupled) * scale[p]).astype(BF16)
+        items = [(p + n, c) for n in range(2) for c in range(coups)]
+        lefts = []
+        for at in range(0, len(items), 4):
+            four = items[at : at + 4]
+            got = four_nn(
+                [margin[n, c, pl.ds(row0, rows), :] for n, c in four],
+                [slots[it][:, couplings_ref[c, n]].reshape(rank, rank) for n, c in four],
+            )
+            lefts += [(weight_ref[c, n] * x).astype(BF16) for (n, c), x in zip(four, got)]
+        two = [jnp.concatenate(lefts[n * coups : (n + 1) * coups], axis=1) for n in range(2)]
+        wide = [
+            jnp.concatenate([margin[p + n, c] for c in range(coups)], axis=1) for n in range(2)
+        ]
+        coupled = dot_nt(jnp.concatenate(two, axis=0), jnp.concatenate(wide, axis=0))
+        parts = (coupled[:rows, :rank], coupled[rows:, rank:])
+        return [
+            ((integ[p + n] - parts[n]) * scale[p + n]).astype(BF16) for n in range(2)
+        ]
 
     def deliver(it):
         e = (it + 1) % 2
@@ -309,11 +351,11 @@
     for it in range(ITERS - 1):
         finish = deliver(it)
 
-        def step(p, carry, it=it):
-            local[p] = relax(it, p)
+        def step(n, carry, it=it):
+            local[2 * n], local[2 * n + 1] = relax(it, 2 * n)
             return carry
 
-        lax.fori_loop(0, pairs, step, 0, unroll=UNROLL)
+        lax.fori_loop(0, pairs // 2, step, 0, unroll=UNROLL // 2)
         finish()
 
     finish = deliver(ITERS - 1)
@@ -350,8 +392,8 @@
         turn_side = lax.rem(side + step, sides)
         chunk = turn_lane * sides + turn_side
         base = chunk * share
-        for k in range(share):
-            afin[rep, base + k] = relax(ITERS - 1, base + k)
+        for k in range(0, share, 2):
+            afin[rep, base + k], afin[rep, base + k + 1] = relax(ITERS - 1, base + k)
         for j in range(1, lanes):
             final_lane(j, chunk).start()
         if sides == 2:

time: 128 us -> 88.7 us (0.69)
  Pallas kernels: 122 us -> 83.4 us
    pallas_call x1, Pallas kernels: 122 us -> 83.4 us  [body(): pl.pallas_call(functools.partial(kernel, groups, reps), out_shape=(jax.Sh...]
where the time goes in v3:
time: 88.7 us; the launch traced here: 88.5 us
  Pallas kernels  83.4 us (94%)
  local copies, waits for them, and re-layouts  3.78 us (4%)
  between operations  1.3 us (1%)
    pallas_call x1, Pallas kernels, body(): pl.pallas_call(functools.partial(kernel, groups, reps), out_shape=(jax.Sh...  83.4 us
    unnamed x2, local copies, waits for them, and re-layouts  3.78 us

profile of v3, /device:TPU:0, one launch (start us, length us, event | category | flops | bytes accessed | tf_op | source)
XLA Modules:
  0.0 88.5 jit_solution(17457264299448210144)
XLA Ops:
  1.3 83.4 %shard_map.122 = (bf16[32,128,128]{2,1,0:T(8,128)(2,1)}, f32[1,128,128]{2,1,0:T(8,128)}) custom-call(bf16[1,128,512]{2,1,0:T(8,128)(2,1)} %factors_ref.1, bf16[1,512,128]{2,1,0:T(8,128)(2,1)} %virtuals_ref.1, bf16[1,1]{1,0:T(2,128)(2,1)} %bitcast.8.occ_ref, f32[32,2,128]{2,1,0:T(2,128)} %energies_ref.1, s32[2,32]{1,0:T(2,128)} %bitcast.11, ...), custom_call_target="tpu_custom_call" | custom-call | flops 1207959552 | bytes 6291456 | tf_op jit(solution)/shard_map/pallas_call | solution.py:548
  84.7 2.3 %copy.16 = bf16[32,128,128]{2,1,0:T(8,128)(2,1)} copy(bf16[32,128,128]{2,1,0:T(8,128)(2,1)} %get-tuple-element.4) | data formatting | bytes 2097152
  87.0 1.5 %copy.17 = f32[1,128,128]{2,1,0:T(8,128)} copy(f32[1,128,128]{2,1,0:T(8,128)} %get-tuple-element.5) | data formatting | bytes 131072

commit v4 on v3

--- a/solution.py
+++ b/solution.py
@@ -10,6 +10,8 @@
 ITERS = 3
 OCC_ROWS = 16
 UNROLL = 8
+HALF_PARTS = 4
+SLOT_PARTS = 2
 F32 = jnp.float32
 BF16 = jnp.bfloat16
 
@@ -67,7 +69,7 @@
     couplings_ref,
     rotations_hbm,
     margins_hbm,
-    amp_ref,
+    amp_hbm,
     dens_ref,
     rot,
     margin,
@@ -86,6 +88,7 @@
     drecv2,
     dfin,
     load_sem,
+    lay_sem,
     s1,
     r1,
     ys,
@@ -159,92 +162,89 @@
     for o in range(orbs):
         half = dot_nn(factors_ref[o], virtuals_ref[o]).astype(BF16)
         level = jnp.broadcast_to(occ_ref[o : o + 1].astype(F32), (OCC_ROWS, rank))
-        halves[0][me * orbs + o, :aux, :] = half
-        halves[0][me * orbs + o, aux:, :] = level.astype(BF16)
+        halves[0][o, :aux, :] = half
+        halves[0][o, aux:, :] = level.astype(BF16)
 
     pl.semaphore_wait(barrier, groups - 1 + reps - 1)
 
     def group_copy(e, k, src, here):
         to = lax.rem(me + k, groups)
-        return send(src(to), here(0, 0, me), s1.at[e, k], r1.at[e, k], to, rep)
-
-    def spread(e, src, here, land, between, ready):
-        def source(k):
-            return lax.rem(me - k + groups, groups)
-
-        def lane_copy(j, k):
-            q = source(k)
+        return send(src(to), here(0, 0, k, 1), s1.at[e, k], r1.at[e, k], to, rep)
+
+    def nearness(index, width):
+        within = lax.rem(index, width)
+        return lax.rem(width * (me + groups) - (index - within), width * groups) + within
+
+    def spread(e, src, here, land, parts, between, ready):
+        parts = parts if groups % parts == 0 else 1
+        size = groups // parts
+
+        def lane_copy(j, n):
+            k = n * size
             return send(
-                here(0, 0, q), land(j, 0, q), ys.at[e, j, k], yr.at[e, j, k], me, lane_rep(j)
+                here(0, 0, k, size),
+                land(j, 0, k, size),
+                ys.at[e, j, n],
+                yr.at[e, j, n],
+                me,
+                lane_rep(j),
             )
 
-        def twin_copy(j, k):
-            q = source(k)
-            return send(here(j, 0, q), land(j, 1, q), ss.at[e, j, k], sr.at[e, j, k], me, twin)
+        def twin_copy(j, n):
+            k = n * size
+            return send(
+                here(j, 0, k, size), land(j, 1, k, size), ss.at[e, j, n], sr.at[e, j, n], me, twin
+            )
 
         def took(place, ssem, rsem):
             send(place, place, ssem, rsem, me, twin).wait_recv()
 
-        def forward(k, carry):
-            for j in range(1, lanes):
-                lane_copy(j, k).start()
-            if sides == 2:
-                twin_copy(0, k).start()
-            return carry
-
         def arrive(k, carry):
             between(k)
-            took(here(0, 0, source(k)), s1.at[e, k], r1.at[e, k])
-            return forward(k, carry)
-
-        forward(0, 0)
-        lax.fori_loop(1, groups, arrive, 0)
+            took(here(0, 0, k, 1), s1.at[e, k], r1.at[e, k])
+            return carry
+
+        for n in range(parts):
+            lax.fori_loop(max(n * size, 1), (n + 1) * size, arrive, 0)
+            for j in range(1, lanes):
+                lane_copy(j, n).start()
+            if sides == 2:
+                twin_copy(0, n).start()
         ready(0, 0)
 
         for j in range(1, lanes):
-
-            def relay(k, carry, j=j):
-                took(here(j, 0, source(k)), ys.at[e, j, k], yr.at[e, j, k])
+            for n in range(parts):
+                took(here(j, 0, n * size, size), ys.at[e, j, n], yr.at[e, j, n])
                 if sides == 2:
-                    twin_copy(j, k).start()
-                return carry
-
-            lax.fori_loop(0, groups, relay, 0)
+                    twin_copy(j, n).start()
             ready(j, 0)
 
         if sides == 2:
             for j in range(lanes):
-
-                def settle(k, carry, j=j):
-                    took(here(j, 1, source(k)), ss.at[e, j, k], sr.at[e, j, k])
-                    return carry
-
-                lax.fori_loop(0, groups, settle, 0)
+                for n in range(parts):
+                    took(here(j, 1, n * size, size), ss.at[e, j, n], sr.at[e, j, n])
                 ready(j, 1)
-
-        def sent(k, carry):
-            for j in range(1, lanes):
-                lane_copy(j, k).wait_send()
-            if sides == 2:
-                for j in range(lanes):
-                    twin_copy(j, k).wait_send()
-            return carry
 
         def sent_group(k, carry):
             group_copy(e, k, src, here).wait_send()
             return carry
 
         def finish():
-            lax.fori_loop(0, groups, sent, 0)
+            for n in range(parts):
+                for j in range(1, lanes):
+                    lane_copy(j, n).wait_send()
+                if sides == 2:
+                    for j in range(lanes):
+                        twin_copy(j, n).wait_send()
             lax.fori_loop(1, groups, sent_group, 0)
 
         return finish
 
-    def half_place(j, t, q):
-        return halves[j * sides + t].at[pl.ds(q * orbs, orbs)]
+    def half_place(j, t, k, n):
+        return halves[j * sides + t].at[pl.ds(k * orbs, n * orbs)]
 
     def half_source(d):
-        return half_place(0, 0, me)
+        return half_place(0, 0, 0, 1)
 
     def start_half(k, carry):
         group_copy(0, k, half_source, half_place).start()
@@ -268,8 +268,8 @@
 
         def step(n, carry):
             four = [4 * n + m for m in range(4)]
-            left = [block[orbitals_ref[0, p]] for p in four]
-            right = [block[orbitals_ref[1, p]] for p in four]
+            left = [block[nearness(orbitals_ref[0, p], orbs)] for p in four]
+            right = [block[nearness(orbitals_ref[1, p], orbs)] for p in four]
             turned = four_nt(
                 [turn[p, pl.ds(row0, rows), :] for p in four], [x[:aux] for x in left]
             )
@@ -297,7 +297,7 @@
 
         lax.fori_loop(0, pairs // 4, step, 0, unroll=2)
 
-    finish = spread(0, half_source, half_place, half_place, flip, integrate)
+    finish = spread(0, half_source, half_place, half_place, HALF_PARTS, flip, integrate)
     margin_copy.wait()
     finish()
 
@@ -308,7 +308,10 @@
             four = items[at : at + 4]
             got = four_nn(
                 [margin[n, c, pl.ds(row0, rows), :] for n, c in four],
-                [slots[it][:, couplings_ref[c, n]].reshape(rank, rank) for n, c in four],
+                [
+                    slots[it][:, nearness(couplings_ref[c, n], capa)].reshape(rank, rank)
+                    for n, c in four
+                ],
             )
             lefts += [(weight_ref[c, n] * x).astype(BF16) for (n, c), x in zip(four, got)]
         two = [jnp.concatenate(lefts[n * coups : (n + 1) * coups], axis=1) for n in range(2)]
@@ -324,12 +327,12 @@
     def deliver(it):
         e = (it + 1) % 2
 
-        def slot_place(j, t, q):
+        def slot_place(j, t, k, n):
             index = lax.rem(lane - j + lanes, lanes) * sides + (side if t == 0 else 1 - side)
-            return slots[it].at[index, pl.ds(q * capa, capa)]
-
-        def slot_land(j, t, q):
-            return slot_place(0 if t == 0 else j, 0, q)
+            return slots[it].at[index, pl.ds(k * capa, n * capa)]
+
+        def slot_land(j, t, k, n):
+            return slot_place(0 if t == 0 else j, 0, k, n)
 
         def slot_source(d):
             return sbuf.at[it, d]
@@ -343,9 +346,15 @@
 
         lax.fori_loop(1, groups, post, 0)
         for s in range(capa):
-            slots[it][rep, me * capa + s] = local[slots_ref[s, me]]
+            slots[it][rep, s] = local[slots_ref[s, me]]
         return spread(
-            e, slot_source, slot_place, slot_land, lambda k: None, lambda j, t: None
+            e,
+            slot_source,
+            slot_place,
+            slot_land,
+            SLOT_PARTS,
+            lambda k: None,
+            lambda j, t: None,
         )
 
     for it in range(ITERS - 1):
@@ -407,15 +416,18 @@
     settle_final(rep)
     base = rep * share
 
-    def gram(k, carry):
-        amp = afin[:, base + k].reshape(rank, rank)
-        side_left = dot_nn(rot[base + k, 0], amp).astype(BF16)
-        side_right = dot_nt(rot[base + k, 1], amp).astype(BF16)
-        grams[2 * k] = dot_nt(side_left, side_left) * (1.0 / rank)
-        grams[2 * k + 1] = dot_nt(side_right, side_right) * (1.0 / rank)
-        return carry
-
-    lax.fori_loop(0, share, gram, 0, unroll=2)
+    def gram(n, carry):
+        four = [4 * n + m for m in range(4)]
+        amps = [afin[:, base + k].reshape(rank, rank) for k in four]
+        left = four_nn([rot[base + k, 0] for k in four], amps)
+        right = four_nt([rot[base + k, 1] for k in four], amps)
+        for s, sides_of in enumerate((left, right)):
+            rounded = [x.astype(BF16) for x in sides_of]
+            for k, x in zip(four, four_nt(rounded, rounded)):
+                grams[2 * k + s] = x * (1.0 / rank)
+        return carry
+
+    lax.fori_loop(0, share // 4, gram, 0, unroll=2)
 
     def collect(o, carry):
         for r in range(reps):
@@ -480,10 +492,10 @@
         settle_final(lax.rem(rep + step, reps))
         return carry
 
-    def lay(p, carry):
-        for r in range(reps):
-            amp_ref[p, r * rows : (r + 1) * rows, :] = afin[r, p]
-        return carry
+    def lay(r):
+        return pltpu.make_async_copy(
+            afin.at[r], amp_hbm.at[:, pl.ds(r * rows, rows), :], lay_sem.at[r]
+        )
 
     def density_last(j):
         to = lax.rem(rep + j, reps)
@@ -492,7 +504,8 @@
     for j in range(1, reps):
         density_last(j).start()
     lax.fori_loop(1, reps, settle_rest, 0)
-    lax.fori_loop(0, pairs, lay, 0, unroll=4)
+    for r in range(reps):
+        lay(r).start()
     for j in range(1, reps):
         block = dfin.at[lax.rem(rep - j + reps, reps)]
         send(block, block, d3s.at[j], d3r.at[j], me, rep).wait_recv()
@@ -500,6 +513,8 @@
         dens_ref[:, r * rows : (r + 1) * rows, :] = dfin[r]
 
     finish()
+    for r in range(reps):
+        lay(r).wait()
     for chunk in range(reps):
         for j in range(1, lanes):
             final_lane(j, chunk).wait_send()
@@ -552,7 +567,7 @@
             jax.ShapeDtypeStruct((orbs, rank, rank), F32),
         ),
         in_specs=[vmem] * 4 + [smem] * 5 + [anywhere] * 2,
-        out_specs=(vmem, vmem),
+        out_specs=(anywhere, vmem),
         scratch_shapes=[
             pltpu.VMEM(pair_rotations.shape, BF16),
             pltpu.VMEM(margins.shape, BF16),
@@ -573,12 +588,13 @@
             pltpu.VMEM((groups, orbs, rows, rank), BF16),
             pltpu.VMEM((reps, orbs, rows, rank), F32),
             dma((2,)),
+            dma((reps,)),
             dma((2, groups)),
             dma((2, groups)),
-            dma((2, lanes, groups)),
-            dma((2, lanes, groups)),
-            dma((2, lanes, groups)),
-            dma((2, lanes, groups)),
+            dma((2, lanes, max(HALF_PARTS, SLOT_PARTS))),
+            dma((2, lanes, max(HALF_PARTS, SLOT_PARTS))),
+            dma((2, lanes, max(HALF_PARTS, SLOT_PARTS))),
+            dma((2, lanes, max(HALF_PARTS, SLOT_PARTS))),
             dma((2 * lanes, reps)),
             dma((2 * lanes, reps)),
             dma((reps,)),

time: 88.7 us -> 88.8 us (level)
  no operation moved by 1% of the time
where the time goes in v4:
time: 88.8 us; the launch traced here: 88.5 us
  Pallas kernels  83.4 us (94%)
  local copies, waits for them, and re-layouts  3.78 us (4%)
  between operations  1.3 us (1%)
    pallas_call x1, Pallas kernels, body(): pl.pallas_call(functools.partial(kernel, groups, reps), out_shape=(jax.Sh...  83.4 us
    unnamed x2, local copies, waits for them, and re-layouts  3.78 us

profile of v4, /device:TPU:0, one launch (start us, length us, event | category | flops | bytes accessed | tf_op | source)
XLA Modules:
  0.0 88.5 jit_solution(3953715618067714310)
XLA Ops:
  1.3 83.4 %shard_map.122 = (bf16[32,128,128]{2,1,0:T(8,128)(2,1)}, f32[1,128,128]{2,1,0:T(8,128)}) custom-call(bf16[1,128,512]{2,1,0:T(8,128)(2,1)} %factors_ref.1, bf16[1,512,128]{2,1,0:T(8,128)(2,1)} %virtuals_ref.1, bf16[1,1]{1,0:T(2,128)(2,1)} %bitcast.8.occ_ref, f32[32,2,128]{2,1,0:T(2,128)} %energies_ref.1, s32[2,32]{1,0:T(2,128)} %bitcast.11, ...), custom_call_target="tpu_custom_call" | custom-call | flops 1207959552 | bytes 6291456 | tf_op jit(solution)/shard_map/pallas_call | solution.py:563
  84.7 2.3 %copy.16 = bf16[32,128,128]{2,1,0:T(8,128)(2,1)} copy(bf16[32,128,128]{2,1,0:T(8,128)(2,1)} %get-tuple-element.4) | data formatting | bytes 2097152
  87.0 1.5 %copy.17 = f32[1,128,128]{2,1,0:T(8,128)} copy(f32[1,128,128]{2,1,0:T(8,128)} %get-tuple-element.5) | data formatting | bytes 131072

commit v5 on v4

--- a/solution.py
+++ b/solution.py
@@ -10,8 +10,8 @@
 ITERS = 3
 OCC_ROWS = 16
 UNROLL = 8
-HALF_PARTS = 4
-SLOT_PARTS = 2
+HALF_PARTS = 8
+SLOT_PARTS = 4
 F32 = jnp.float32
 BF16 = jnp.bfloat16
 
@@ -299,7 +299,6 @@
 
     finish = spread(0, half_source, half_place, half_place, HALF_PARTS, flip, integrate)
     margin_copy.wait()
-    finish()
 
     def relax(it, p):
         items = [(p + n, c) for n in range(2) for c in range(coups)]
@@ -324,7 +323,7 @@
             ((integ[p + n] - parts[n]) * scale[p + n]).astype(BF16) for n in range(2)
         ]
 
-    def deliver(it):
+    def deliver(it, earlier):
         e = (it + 1) % 2
 
         def slot_place(j, t, k, n):
@@ -354,20 +353,19 @@
             slot_land,
             SLOT_PARTS,
             lambda k: None,
-            lambda j, t: None,
+            lambda j, t: earlier() if j == 0 and t == 0 else None,
         )
 
     for it in range(ITERS - 1):
-        finish = deliver(it)
+        finish = deliver(it, finish)
 
         def step(n, carry, it=it):
             local[2 * n], local[2 * n + 1] = relax(it, 2 * n)
             return carry
 
         lax.fori_loop(0, pairs // 2, step, 0, unroll=UNROLL // 2)
-        finish()
-
-    finish = deliver(ITERS - 1)
+
+    finish = deliver(ITERS - 1, finish)
 
     def piece(r, chunk):
         return afin.at[r, pl.ds(chunk * share, share)]
@@ -530,6 +528,21 @@
         return carry
 
     lax.fori_loop(1, groups, sent_density, 0)
+
+
+def hand_over(reps, amp_in, dens_in, amp_out, dens_out, sem):
+    part = amp_in.shape[0] // reps
+    copies = [
+        pltpu.make_async_copy(
+            amp_in.at[pl.ds(r * part, part)], amp_out.at[pl.ds(r * part, part)], sem.at[r]
+        )
+        for r in range(reps)
+    ]
+    copies.append(pltpu.make_async_copy(dens_in, dens_out, sem.at[reps]))
+    for copy in copies:
+        copy.start()
+    for copy in copies:
+        copy.wait()
 
 
 def body(
@@ -560,7 +573,7 @@
     smem = pl.BlockSpec(memory_space=pltpu.SMEM)
     anywhere = pl.BlockSpec(memory_space=pl.ANY)
     dma = pltpu.SemaphoreType.DMA
-    return pl.pallas_call(
+    results = pl.pallas_call(
         functools.partial(kernel, groups, reps),
         out_shape=(
             jax.ShapeDtypeStruct((pairs, rank, rank), BF16),
@@ -625,6 +638,14 @@
         pair_rotations,
         margins,
     )
+    return pl.pallas_call(
+        functools.partial(hand_over, reps),
+        out_shape=tuple(jax.ShapeDtypeStruct(x.shape, x.dtype) for x in results),
+        in_specs=[anywhere] * 2,
+        out_specs=(anywhere, anywhere),
+        scratch_shapes=[dma((reps + 1,))],
+        compiler_params=pltpu.CompilerParams(vmem_limit_bytes=60 * 1024 * 1024),
+    )(*results)
 
 
 def solution(mesh):

time: 88.8 us -> 119 us (1.34)
  Pallas kernels: 83.4 us -> 118 us
  local copies, waits for them, and re-layouts: 3.78 us -> 0 us
    pallas_call x0 -> x1, Pallas kernels: none -> 34.9 us  [body(): pl.pallas_call(functools.partial(hand_over, reps), out_shape=tuple((jax.S...]
    unnamed x2 -> x0, local copies, waits for them, and re-layouts: 3.78 us -> none
where the time goes in v5:
time: 119 us
  Pallas kernels  118 us (99%)
  between operations  1.29 us (1%)
    pallas_call x1, Pallas kernels, body(): pl.pallas_call(functools.partial(kernel, groups, reps), out_shape=(jax.Sh...  82.8 us
    pallas_call x1, Pallas kernels, body(): pl.pallas_call(functools.partial(hand_over, reps), out_shape=tuple((jax.S...  34.9 us

profile of v5, /device:TPU:0, one launch (start us, length us, event | category | flops | bytes accessed | tf_op | source)
XLA Modules:
  0.0 119.0 jit_solution(5923986296144471876)
XLA Ops:
  1.3 82.8 %shard_map.122 = (bf16[32,128,128]{2,1,0:T(8,128)(2,1)}, f32[1,128,128]{2,1,0:T(8,128)}) custom-call(bf16[1,128,512]{2,1,0:T(8,128)(2,1)} %factors_ref.1, bf16[1,512,128]{2,1,0:T(8,128)(2,1)} %virtuals_ref.1, bf16[1,1]{1,0:T(2,128)(2,1)} %bitcast.8.occ_ref, f32[32,2,128]{2,1,0:T(2,128)} %energies_ref.1, s32[2,32]{1,0:T(2,128)} %bitcast.11, ...), custom_call_target="tpu_custom_call" | custom-call | flops 1207959552 | bytes 6291456 | tf_op jit(solution)/shard_map/pallas_call | solution.py:576
  84.1 34.9 %shard_map.123 = (bf16[32,128,128]{2,1,0:T(8,128)(2,1)}, f32[1,128,128]{2,1,0:T(8,128)}) custom-call(bf16[32,128,128]{2,1,0:T(8,128)(2,1)} %get-tuple-element.4.amp_in, f32[1,128,128]{2,1,0:T(8,128)} %get-tuple-element.5.dens_in), custom_call_target="tpu_custom_call" | custom-call | tf_op jit(solution)/shard_map/pallas_call | solution.py:641

commit v6 on v5

--- a/solution.py
+++ b/solution.py
@@ -530,19 +530,9 @@
     lax.fori_loop(1, groups, sent_density, 0)
 
 
-def hand_over(reps, amp_in, dens_in, amp_out, dens_out, sem):
-    part = amp_in.shape[0] // reps
-    copies = [
-        pltpu.make_async_copy(
-            amp_in.at[pl.ds(r * part, part)], amp_out.at[pl.ds(r * part, part)], sem.at[r]
-        )
-        for r in range(reps)
-    ]
-    copies.append(pltpu.make_async_copy(dens_in, dens_out, sem.at[reps]))
-    for copy in copies:
-        copy.start()
-    for copy in copies:
-        copy.wait()
+def hand_over(amp_in, dens_in, amp_out, dens_out):
+    amp_out[...] = amp_in[...]
+    dens_out[...] = dens_in[...]
 
 
 def body(
@@ -639,11 +629,10 @@
         margins,
     )
     return pl.pallas_call(
-        functools.partial(hand_over, reps),
+        hand_over,
         out_shape=tuple(jax.ShapeDtypeStruct(x.shape, x.dtype) for x in results),
-        in_specs=[anywhere] * 2,
-        out_specs=(anywhere, anywhere),
-        scratch_shapes=[dma((reps + 1,))],
+        in_specs=[vmem] * 2,
+        out_specs=(vmem, vmem),
         compiler_params=pltpu.CompilerParams(vmem_limit_bytes=60 * 1024 * 1024),
     )(*results)
 

time: 119 us -> 86.5 us (0.73)
  Pallas kernels: 118 us -> 85.1 us
    pallas_call x1, Pallas kernels: 34.9 us -> 2.27 us  [body(): pl.pallas_call(hand_over, out_shape=tuple((jax.ShapeDtypeStruct(x.shape,...]
where the time goes in v6:
time: 86.5 us; the launch traced here: 86.3 us
  Pallas kernels  85.1 us (98%)
  between operations  1.29 us (1%)
    pallas_call x1, Pallas kernels, body(): pl.pallas_call(functools.partial(kernel, groups, reps), out_shape=(jax.Sh...  82.8 us
    pallas_call x1, Pallas kernels, body(): pl.pallas_call(hand_over, out_shape=tuple((jax.ShapeDtypeStruct(x.shape,...  2.27 us

profile of v6, /device:TPU:0, one launch (start us, length us, event | category | flops | bytes accessed | tf_op | source)
XLA Modules:
  0.0 86.3 jit_solution(14605118508079226019)
XLA Ops:
  1.3 82.8 %shard_map.122 = (bf16[32,128,128]{2,1,0:T(8,128)(2,1)}, f32[1,128,128]{2,1,0:T(8,128)}) custom-call(bf16[1,128,512]{2,1,0:T(8,128)(2,1)} %factors_ref.1, bf16[1,512,128]{2,1,0:T(8,128)(2,1)} %virtuals_ref.1, bf16[1,1]{1,0:T(2,128)(2,1)} %bitcast.8.occ_ref, f32[32,2,128]{2,1,0:T(2,128)} %energies_ref.1, s32[2,32]{1,0:T(2,128)} %bitcast.11, ...), custom_call_target="tpu_custom_call" | custom-call | flops 1207959552 | bytes 6291456 | tf_op jit(solution)/shard_map/pallas_call | solution.py:566
  84.1 2.3 %shard_map.123 = (bf16[32,128,128]{2,1,0:T(8,128)(2,1)}, f32[1,128,128]{2,1,0:T(8,128)}) custom-call(bf16[32,128,128]{2,1,0:T(8,128)(2,1)} %get-tuple-element.4.amp_in, f32[1,128,128]{2,1,0:T(8,128)} %get-tuple-element.5.dens_in), custom_call_target="tpu_custom_call" | custom-call | tf_op jit(solution)/shard_map/pallas_call | solution.py:631
